TPU v7x, 512 devices: a whole 4x4x16 slice. The times are simulated.
512 devices in a mesh: tok: 32 (over z, x_hi), ch: 16 (over x_lo, y, core).
Axes of the slice: x: 4 (x_hi: 2, x_lo: 2; x = x_hi * 2 + x_lo), y: 4, z: 16, core: 2. Of those that a mesh axis runs over, the one named last changes fastest.
Arguments:
- tokens: bfloat16 [4096, 4096], P('tok', 'ch'), may hold values from -6 to 6
- w_input: bfloat16 [4096, 8192], P('tok', 'ch'), may hold values from -0.09375 to 0.09375
- cotangent: bfloat16 [4096, 8192], P('tok', 'ch'), may hold values from -6 to 6
- b_state: bfloat16 [8, 4096, 128], P(None, 'tok'), may hold values from -0.1875 to 0.1875
- c_state: bfloat16 [8, 4096, 128], P(None, 'tok'), may hold values from -0.1875 to 0.1875
- step_raw: float32 [128, 4096], P('ch', 'tok'), as said below
- rate_log: float32 [128], P('ch'), as said below
- skip_gain: float32 [128], P('ch'), may hold values from 0.5 to 1.5
Outputs:
- token_grad: bfloat16 [4096, 4096], P('tok', 'ch')
- weight_grad: bfloat16 [4096, 8192], P('tok', 'ch')
- step_grad: float32 [128, 4096], P('ch', 'tok')
- output_map_grad: float32 [8, 4096, 128], P(None, 'tok')
Inputs may be any that keep to these rules, and one draw needn't show every extreme that they name: `rate_log`: every value lies between log(0.3 / 4096) and log(0.05). `step_raw`: every value lies between -2.5 and 3.5.
All inputs are finite; a program needn't handle non-finite values.
Results may differ from a plain program's by a relative error of at most 0.025.
Values may be sent and summed in bfloat16 or wider, within the bound.
A program may use at most 128 MiB of HBM per device.

v0:
```python
import jax
import jax.numpy as jnp
from jax import lax
from jax.sharding import PartitionSpec as P

HEADS = 128
HEAD_DIM = 64
GROUPS = 8


highest = lax.Precision.HIGHEST


def prefix(array, axis, combine, identity, reverse):
    count, place = (lax.axis_size(axis), lax.axis_index(axis))
    everything = jax.tree.map(
        lambda part, kind: lax.all_gather(part.astype(kind), axis),
        array,
        (jnp.bfloat16, jnp.bfloat16),
    )
    start = jax.tree.map(
        lambda part, zero: jnp.broadcast_to(jnp.asarray(zero, part.dtype), part.shape),
        array,
        identity,
    )

    def hop(k, before):
        at = count - 1 - k if reverse else k
        reached = at > place if reverse else at < place
        new = combine(
            before, jax.tree.map(lambda part, own: part[at].astype(own.dtype), everything, array)
        )
        return jax.tree.map(lambda a, b: jnp.where(reached, a, b), new, before)

    return lax.fori_loop(0, count, hop, start)


def block_local(inputs_h, grad_h, b_heads, c_heads, steps, rates):
    log_decay = jnp.cumsum(steps * rates[:, None], axis=1)
    log_total = log_decay[:, -1:]
    end_weight = jnp.exp(log_total - log_decay) * steps
    block_decay = jnp.exp(log_total[:, 0])
    state_local = jnp.einsum("lhp,hl,hln->hpn", inputs_h, end_weight, b_heads, precision=highest)
    adjoint_local = jnp.einsum(
        "lhp,hl,hln->hpn", grad_h, jnp.exp(log_decay), c_heads, precision=highest
    )
    return (block_decay, state_local, adjoint_local)


def block_grads(
    inputs_h,
    grad_h,
    inputs_low,
    grad_low,
    b_heads,
    c_heads,
    b_low,
    c_low,
    steps,
    step_raw,
    rates,
    skip_gain,
    state_in,
    adjoint_in,
):
    length = steps.shape[1]
    log_decay = jnp.cumsum(steps * rates[:, None], axis=1)
    log_total = log_decay[:, -1:]
    end_weight = jnp.exp(log_total - log_decay) * steps
    row_ids = jnp.arange(length)[:, None]
    col_ids = jnp.arange(length)[None, :]
    lower_mask = row_ids >= col_ids
    log_gap = log_decay[:, :, None] - log_decay[:, None, :]
    decay_mat = jnp.where(lower_mask[None], jnp.exp(jnp.minimum(log_gap, 0.0)), 0.0)
    intersection = jnp.einsum("hrn,hsn->hrs", c_low, b_low, preferred_element_type=jnp.float32)
    kernel = decay_mat * intersection
    adjoint_b = jnp.einsum("hpn,hsn->shp", adjoint_in, b_heads, precision=highest)
    back_proj = jnp.einsum("hrs,rhp->shp", kernel, grad_h, precision=highest)
    back_proj = back_proj + jnp.exp(log_total - log_decay).T[:, :, None] * adjoint_b
    input_grad = skip_gain[None, :, None] * grad_h + steps.T[:, :, None] * back_proj
    input_term = jnp.sum(inputs_h * back_proj, axis=-1).T
    cross = jnp.einsum("rhp,shp->hrs", grad_low, inputs_low, preferred_element_type=jnp.float32)
    pair_weights = decay_mat * steps[:, None, :] * cross
    map_local = jnp.einsum("hts,hsn->htn", pair_weights, b_heads, precision=highest)
    state_g = jnp.einsum("hpn,thp->htn", state_in, grad_h, precision=highest)
    map_heads = map_local + jnp.exp(log_decay)[:, :, None] * state_g
    pair_terms = kernel * steps[:, None, :] * cross
    upper_ones = (col_ids >= row_ids).astype(jnp.float32)
    strict_lower = (col_ids < row_ids).astype(jnp.float32)
    tail_sums = jnp.einsum("tr,hrs->hts", upper_ones, pair_terms, precision=highest)
    pair_part = jnp.sum(tail_sums * strict_lower[None], axis=-1)
    state_c = jnp.einsum("hpn,hrn->rhp", state_in, c_heads, precision=highest)
    start_terms = jnp.exp(log_decay) * jnp.sum(grad_h * state_c, axis=-1).T
    start_part = jnp.einsum("tr,hr->ht", upper_ones, start_terms, precision=highest)
    end_terms = end_weight * jnp.sum(inputs_h * adjoint_b, axis=-1).T
    end_part = jnp.einsum("ts,hs->ht", strict_lower, end_terms, precision=highest)
    corner = jnp.exp(log_total[:, 0]) * jnp.sum(adjoint_in * state_in, axis=(1, 2))
    decay_term = pair_part + start_part + end_part + corner[:, None]
    step_grad = jax.nn.sigmoid(step_raw) * (input_term + rates[:, None] * decay_term)
    return (input_grad, step_grad, map_heads)


def join_states(earlier, later):
    return (earlier[0] * later[0], later[0][:, None, None] * earlier[1] + later[1])


def local(tokens, w_input, cotangent, b_state, c_state, step_raw, rate_log, skip_gain):
    length = tokens.shape[0]
    heads_here = step_raw.shape[0]
    width_here = w_input.shape[1]
    groups = b_state.shape[0]
    per_group = HEADS // GROUPS
    features = lax.all_gather(tokens, "ch", axis=1, tiled=True)
    inputs = jnp.dot(
        features,
        lax.all_gather(w_input, "tok", axis=0, tiled=True),
        preferred_element_type=jnp.float32,
    )
    inputs = inputs.astype(jnp.bfloat16)
    inputs_low = inputs.reshape(length, heads_here, HEAD_DIM)
    grad_low = cotangent.reshape(length, heads_here, HEAD_DIM)
    inputs_h = inputs_low.astype(jnp.float32)
    grad_h = grad_low.astype(jnp.float32)
    head_ids = lax.axis_index("ch") * heads_here + jnp.arange(heads_here, dtype=jnp.int32)
    group_ids = head_ids // per_group
    one_hot = (group_ids[:, None] == jnp.arange(groups, dtype=jnp.int32)[None, :]).astype(
        jnp.bfloat16
    )
    b_low = jnp.einsum("hg,gln->hln", one_hot, b_state, preferred_element_type=jnp.float32).astype(
        jnp.bfloat16
    )
    c_low = jnp.einsum("hg,gln->hln", one_hot, c_state, preferred_element_type=jnp.float32).astype(
        jnp.bfloat16
    )
    b_heads = b_low.astype(jnp.float32)
    c_heads = c_low.astype(jnp.float32)
    steps = jax.nn.softplus(step_raw)
    rates = -jnp.exp(rate_log)
    block_decay, state_local, adjoint_local = block_local(
        inputs_h, grad_h, b_heads, c_heads, steps, rates
    )
    identity = (jnp.ones((heads_here,), jnp.float32), jnp.zeros_like(state_local))
    state_in = prefix((block_decay, state_local), "tok", join_states, identity, False)[1]
    adjoint_in = prefix((block_decay, adjoint_local), "tok", join_states, identity, True)[1]
    input_grad, step_grad, map_heads = block_grads(
        inputs_h,
        grad_h,
        inputs_low,
        grad_low,
        b_heads,
        c_heads,
        b_low,
        c_low,
        steps,
        step_raw,
        rates,
        skip_gain,
        state_in,
        adjoint_in,
    )
    map_terms = jnp.einsum("hg,htn->gtn", one_hot.astype(jnp.float32), map_heads, precision=highest)
    output_map_grad = lax.psum(map_terms.astype(jnp.bfloat16), "ch").astype(jnp.float32)
    input_grad = input_grad.reshape(length, width_here).astype(jnp.bfloat16)
    partial_grad = lax.dot_general(
        input_grad,
        lax.all_gather(w_input, "tok", axis=0, tiled=True),
        (((1,), (1,)), ((), ())),
        preferred_element_type=jnp.float32,
    )
    token_grad = lax.psum_scatter(
        partial_grad.astype(jnp.bfloat16), "ch", scatter_dimension=1, tiled=True
    )
    feature_columns = lax.all_to_all(features, "tok", split_axis=1, concat_axis=0, tiled=True)
    weight_grad = lax.dot_general(
        feature_columns,
        lax.all_gather(input_grad, "tok", axis=0, tiled=True),
        (((0,), (0,)), ((), ())),
        preferred_element_type=jnp.float32,
    )
    return (token_grad, weight_grad.astype(jnp.bfloat16), step_grad, output_map_grad)


def solution(mesh):
    placed = (
        P("tok", "ch"),
        P("tok", "ch"),
        P("tok", "ch"),
        P(None, "tok", None),
        P(None, "tok", None),
        P("ch", "tok"),
        P("ch"),
        P("ch"),
    )
    return jax.shard_map(
        local,
        mesh=mesh,
        in_specs=placed,
        out_specs=(P("tok", "ch"), P("tok", "ch"), P("ch", "tok"), P(None, "tok", None)),
        check_vma=False,
    )
```

profile of v0, /device:TPU:1, one launch (start us, length us, event | category | flops | bytes accessed | tf_op | source)
XLA Modules:
  0.0 932.4 jit_solution(9311608605607458388)
XLA Ops:
  7.2 1.6 copy.84
  9.7 1.0 copy.74
  13.8 1.1 fusion.9
  15.0 1.3 dynamic-slice
  17.3 70.8 %all-reduce = bf16[256]{0:T(256)(128)(2,1)S(1)} all-reduce(bf16[256]{0:T(256)(128)(2,1)S(1)} %dynamic-update-slice), channel_id=2, replica_groups=mesh['tok'=32,'ch'=16] {'tok'}, use_global_device_ids=true, to_apply=%add | all-reduce | flops 256 | bytes 1024
  88.3 2.1 convert_multiply_fusion
  90.7 6.5 all-to-all-start
  97.2 131.6 %all-gather.9.cloned.1.call-done = bf16[4096,512]{1,0:T(8,128)(2,1)} async-done(((bf16[128,512]{1,0:T(8,128)(2,1)}), bf16[4096,512]{1,0:T(8,128)(2,1)}) %all-gather.9.cloned.1.call-update) | async-done | bytes 4194320 | tf_op jit(solution)/shard_map/all_gather | solution.py:166
  228.9 3.3 convolution_convert_fusion.5
  232.6 2.1 convolution_convert_fusion.4
  234.7 156.5 %all-gather.15.cloned.1.call-done = bf16[256,64,128]{2,1,0:T(8,128)(2,1)} async-done(((bf16[8,64,128]{2,1,0:T(8,128)(2,1)}), bf16[256,64,128]{2,1,0:T(8,128)(2,1)}) %all-gather.15.cloned.1.call-update) | async-done | bytes 4194320 | tf_op jit(solution)/shard_map/all_gather | solution.py:17
  391.3 34.1 %while.30 = (s32[]{:T(128)}, f32[8,64,128]{2,1,0:T(8,128)S(1)}, s32[]{:T(128)}, bf16[32,8]{1,0:T(8,128)(2,1)S(1)}, bf16[32,8,64,128]{3,2,1,0:T(8,128)(2,1)}, /*index=5*/s32[]{:T(128)}, s32[]{:T(128)}, s32[]{:T(128)}, s32[]{:T(128)}) while((s32[]{:T(128)}, f32[8,64,128]{2,1,0:T(8,128)S(1)}, s32[]{:T(128)}, ...), condition=%wide.region_2.3_spmd.clone, body=%wide.region_1.2_spmd.clone.sunk | while | flops 327696 | bytes 655615 | solution.py:35
  393.4 1.0 fusion.74
  395.5 1.0 fusion.74
  397.7 1.0 fusion.74
  399.8 1.0 fusion.74
  419.0 1.0 fusion.74
  424.3 1.0 fusion.74
  426.0 1.1 fusion.25
  427.1 1.3 fusion.18
  428.4 124.4 %all-gather.17.cloned.1.call-done = bf16[256,64,128]{2,1,0:T(8,128)(2,1)} async-done(((bf16[8,64,128]{2,1,0:T(8,128)(2,1)}), bf16[256,64,128]{2,1,0:T(8,128)(2,1)}) %all-gather.17.cloned.1.call-update) | async-done | bytes 4194320 | tf_op jit(solution)/shard_map/all_gather | solution.py:17
  552.8 33.9 %while.31 = (s32[]{:T(128)}, f32[8,64,128]{2,1,0:T(8,128)S(1)}, s32[]{:T(128)}, bf16[32,8]{1,0:T(8,128)(2,1)S(1)}, bf16[32,8,64,128]{3,2,1,0:T(8,128)(2,1)}, /*index=5*/s32[]{:T(128)}, s32[]{:T(128)}) while((s32[]{:T(128)}, f32[8,64,128]{2,1,0:T(8,128)S(1)}, s32[]{:T(128)}, bf16[32,8]{1,0:T(8,128)(2,1)S(1)}, ...), condition=%wide.region_7.8_spmd.clone, body=%wide.region_6.7_spmd.clone.sunk | while | flops 327692 | bytes 655553 | solution.py:35
  575.0 1.0 fusion.75
  586.7 1.5 fusion.4
  588.2 1.4 convolution_convert_fusion.1
  589.6 4.8 convolution_convert_fusion
  594.4 1.3 copy.85
  596.4 120.1 %all-gather.11.cloned.1.call-done = bf16[4096,512]{0,1:T(8,128)(2,1)} async-done(((bf16[128,512]{0,1:T(8,128)(2,1)}), bf16[4096,512]{0,1:T(8,128)(2,1)}) %all-gather.11.cloned.1.call-update) | async-done | bytes 4194320 | tf_op jit(solution)/shard_map/all_gather | solution.py:176
  716.4 3.7 fusion.10
  723.0 131.1 %all-reduce.3.cloned.1.call-done = bf16[8,128,128]{2,0,1:T(8,128)(2,1)} async-done(((bf16[8,128,128]{2,0,1:T(8,128)(2,1)}), bf16[8,128,128]{2,0,1:T(8,128)(2,1)}) %all-reduce.3.cloned.1.call-update) | async-done | bytes 262160 | tf_op jit(solution)/shard_map/psum | solution.py:162
  854.1 1.8 copy.97
  855.8 69.7 %reduce-scatter.2.cloned.1.call-done = bf16[128,256]{1,0:T(8,128)(2,1)} async-done(((bf16[128,4096]{1,0:T(8,128)(2,1)}), bf16[128,256]{1,0:T(8,128)(2,1)}) %reduce-scatter.2.cloned.1.call-update) | async-done | bytes 65552 | tf_op jit(solution)/shard_map/reduce_scatter | solution.py:170
  (178 shorter events, 68.0 us)
Async XLA Ops:
  7.2 6.3 copy-start
  7.2 83.5 %all-gather.13.cloned.1.call-start = ((), (), s32[]{:S(2)}) async-start(), calls=%async_computation.5 | async-start | bytes 1114112 | tf_op jit(solution)/shard_map/all_gather | solution.py:113
  8.9 220.0 %all-gather.9.cloned.1.call-start = ((), (), s32[]{:S(2)}) async-start(), calls=%async_computation.2 | async-start | bytes 4325376 | tf_op jit(solution)/shard_map/all_gather | solution.py:166
  9.6 381.7 %all-gather.15.cloned.1.call-start = ((), (), s32[]{:S(2)}) async-start(), calls=%async_computation.7 | async-start | bytes 4325376 | tf_op jit(solution)/shard_map/all_gather | solution.py:17
  13.8 76.9 %copy-start.2 = (bf16[8,128,128]{2,0,1:T(8,128)(2,1)}, bf16[8,128,128]{2,0,1:T(8,128)(2,1)S(1)}, u32[]{:S(2)}) copy-start(bf16[8,128,128]{2,0,1:T(8,128)(2,1)S(1)} %get-tuple-element.313) | copy-start | bytes 786436
  90.7 503.7 %all-to-all-start = ((bf16[128,32,128]{0,2,1:T(8,128)(2,1)}), bf16[128,32,128]{0,2,1:T(8,128)(2,1)S(1)}, u32[]{:S(2)}, u32[]{:S(2)}) async-start(bf16[128,32,128]{0,2,1:T(8,128)(2,1)} %bitcast.109), calls=%async_computation.1 | async-start | bytes 2097152 | tf_op jit(solution)/shard_map/all_to_all | solution.py:173
  97.2 455.6 %all-gather.17.cloned.1.call-start = ((), (), s32[]{:S(2)}) async-start(), calls=%async_computation.8 | async-start | bytes 4325376 | tf_op jit(solution)/shard_map/all_gather | solution.py:17
  232.1 193.8 %copy-start.5 = (f32[8]{0:T(128)S(1)}, f32[8]{0:T(128)}, u32[]{:S(2)}) copy-start(f32[8]{0:T(128)} %param.19) | copy-start | bytes 100
  234.7 481.7 %all-gather.11.cloned.1.call-start = ((), (), s32[]{:S(2)}) async-start(), calls=%async_computation.4 | async-start | bytes 4325376 | tf_op jit(solution)/shard_map/all_gather | solution.py:176
  427.0 162.6 %copy-start.1 = (bf16[128,8,64]{0,2,1:T(8,128)(2,1)S(1)}, bf16[128,8,64]{0,2,1:T(8,128)(2,1)}, u32[]{:S(2)}) copy-start(bf16[128,8,64]{0,2,1:T(8,128)(2,1)} %get-tuple-element.306) | copy-start | bytes 393220
  427.1 427.0 %all-reduce.3.cloned.1.call-start = ((), (), s32[]{:S(2)}) async-start(), calls=%async_computation.6 | async-start | bytes 524288 | tf_op jit(solution)/shard_map/psum | solution.py:162
  589.6 335.9 %reduce-scatter.2.cloned.1.call-start = ((), (), s32[]{:S(2)}) async-start(), calls=%async_computation.3 | async-start | bytes 1114112 | tf_op jit(solution)/shard_map/reduce_scatter | solution.py:170
  595.8 125.6 %copy-start.3 = (bf16[8,128,128]{2,0,1:T(8,128)(2,1)S(1)}, bf16[8,128,128]{2,0,1:T(8,128)(2,1)}, u32[]{:S(2)}) copy-start(bf16[8,128,128]{2,0,1:T(8,128)(2,1)} %copy-done.2) | copy-start | bytes 786436
  595.8 126.4 %copy-start.4 = (f32[8,128]{1,0:T(8,128)S(1)}, f32[8,128]{1,0:T(8,128)}, u32[]{:S(2)}) copy-start(f32[8,128]{1,0:T(8,128)} %param.17) | copy-start | bytes 12292
Sparse Core Ops, SparseCore 0:
  10.7 45.7 all-gather.12
  59.7 169.1 all-gather.8
  232.6 158.6 all-gather.14
  394.2 158.5 all-gather.16
  556.1 160.2 all-gather.10
  719.8 134.2 all-reduce.2
  857.7 67.7 reduce-scatter.1
where the time goes:
time: 935 us; the launch traced here: 932 us
  waiting for transfers between devices  734 us (79%)
  blocking collectives  70.8 us (8%)
  other arithmetic  68.6 us (7%)
  matrix products  26 us (3%)
  between operations  15 us (2%)
    all_gather x2, waiting for transfers between devices, prefix(): lax.all_gather(part.astype(kind), axis)  281 us
    all_gather x1, waiting for transfers between devices, local(): lax.all_gather(w_input, 'tok', axis=0, tiled=True)  132 us
    psum x1, waiting for transfers between devices, local(): lax.psum(map_terms.astype(jnp.bfloat16), 'ch').astype(jnp.float32)  131 us
    all_gather x1, waiting for transfers between devices, local(): lax.all_gather(input_grad, 'tok', axis=0, tiled=True)  120 us
    unnamed x1, blocking collectives  70.8 us
    reduce_scatter x1, waiting for transfers between devices, local(): lax.psum_scatter(partial_grad.astype(jnp.bfloat16), 'ch', scatter_dimensi...  69.7 us
    select_n x64, other arithmetic, hop(): return jax.tree.map(lambda a, b: jnp.where(reached, a, b), new, before)  64.9 us
  transfers between devices with their start and end apart: 8, of which 6 were waited for; matrix products, arithmetic and copies ran while one was open for 11% of the time, Pallas kernels for 0%

commit v1 on v0

v1 whole, which is shorter than its diff:
```python
import jax
import jax.numpy as jnp
from jax import lax
from jax.experimental import pallas as pl
from jax.experimental.pallas import tpu as pltpu
from jax.sharding import PartitionSpec as P

MESH = pl.DeviceIdType.MESH
HIGHEST = lax.Precision.HIGHEST
F32 = jnp.float32
BF16 = jnp.bfloat16
TOK = 128
HEAD = 64
HALF = 4
CH = HALF * HEAD
STATE = 128

NN = (((1,), (0,)), ((), ()))
NT = (((1,), (1,)), ((), ()))


def dot(a, b, dims=NN):
    return lax.dot_general(a, b, dims, preferred_element_type=F32)


def dot2(a, b, dims=NN):
    high = a.astype(BF16)
    low = (a - high.astype(F32)).astype(BF16)
    return dot(high, b, dims) + dot(low, b, dims)


def dot_exact(a, b):
    return lax.dot_general(a, b, NN, precision=HIGHEST, preferred_element_type=F32)


def heads_to_rows(rows, p):
    return jnp.concatenate(
        [
            jnp.broadcast_to(rows[p * HALF + i : p * HALF + i + 1], (HEAD, rows.shape[1]))
            for i in range(HALF)
        ],
        axis=0,
    )


def kernel(
    nz,
    nk,
    tokens,
    w,
    cot,
    b_in,
    c_in,
    raw_in,
    rate_log,
    skip_in,
    token_grad,
    weight_grad,
    step_grad,
    map_grad,
    feat,
    wg,
    ig,
    tcol,
    g,
    bs,
    cs,
    raw,
    dtile,
    dall,
    send_state,
    recv_state,
    back_state,
    state_in,
    adj_in,
    gte,
    gtb,
    xtb,
    dec,
    inter,
    back_local,
    abt,
    a_last,
    s_first,
    vecs,
    igtm,
    y_all,
    y_sib,
    y_out,
    y_in,
    m_own,
    m_in,
    m_groups,
    s_out,
    s_swap,
    wgrad,
    local_sem,
    send_sem,
    recv_sem,
):
    tok, c = lax.axis_index("tok"), lax.axis_index("ch")
    z, r = tok // 2, tok % 2
    k, core = c // 2, c % 2
    piece = CH // nz
    rowt = TOK // nk
    chips = 2 * nk

    def ztok(zz, rr):
        return lax.rem(zz + nz, nz) * 2 + rr

    def xor(a, b, n):
        out, bit = 0, 1
        while bit < n:
            pa, pb = (a // bit) % 2, (b // bit) % 2
            out = out + bit * ((pa + pb) % 2)
            bit *= 2
        return out

    def chip(j):
        return (r + j // nk) % 2, xor(k, j % nk, nk)

    slots = {}
    used = [0]

    def slot(name, n):
        if name not in slots:
            slots[name] = used[0]
            used[0] += n
        return slots[name]

    def remote(src, dst, s, tok_to, ch_to):
        return pltpu.make_async_remote_copy(
            src_ref=src,
            dst_ref=dst,
            send_sem=send_sem.at[s],
            recv_sem=recv_sem.at[s],
            device_id=(tok_to, ch_to),
            device_id_type=MESH,
        )

    def each(first, last, f):
        def body(j, carry):
            f(j)
            return carry

        lax.fori_loop(first, last, body, 0)

    class Family:
        def __init__(self, name, first, last, make):
            self.base, self.first, self.last = slot(name, last), first, last
            self.make = lambda j: make(j, self.base + j)

        def start(self):
            each(self.first, self.last, lambda j: self.make(j).start())

        def start_one(self, j):
            self.make(j).start()

        def recv(self):
            each(self.first, self.last, lambda j: self.make(j).wait_recv())

        def recv_one(self, j):
            self.make(j).wait_recv()

        def sent(self):
            each(self.first, self.last, lambda j: self.make(j).wait_send())

    class Ring:
        def __init__(self, name, buf):
            self.base = slot(name, 4 * (nz // 2 + 1))
            self.buf = buf

        def copy(self, way, s, h):
            block = lax.rem(z - way * (s - 1) + 2 * nz, nz)
            at = self.buf.at[block, h]
            sem = self.base + (s * 2 + (0 if way == 1 else 1)) * 2 + h
            return remote(at, at, sem, ztok(z + way, r), c)

        def has(self, way, s, h):
            if s < nz // 2:
                return True
            return s == nz // 2 and h == (0 if way == 1 else 1)

        def begin(self, h):
            for way in (1, -1):
                self.copy(way, 1, h).start()

        def tick(self, s, h):
            for way in (1, -1):
                if self.has(way, s, h):
                    self.copy(way, s, h).wait_recv()
                    if self.has(way, s + 1, h):
                        self.copy(way, s + 1, h).start()

        def both(self, s):
            self.tick(s, 0)
            self.tick(s, 1)

        def sent(self):
            for s in range(1, nz // 2 + 1):
                for h in range(2):
                    for way in (1, -1):
                        if self.has(way, s, h):
                            self.copy(way, s, h).wait_send()

    barrier = pltpu.get_barrier_semaphore()

    def greet(tok_to, ch_to):
        pl.semaphore_signal(barrier, inc=1, device_id=(tok_to, ch_to), device_id_type=MESH)

    def greet_chip(j):
        rr, kk = chip(j)
        greet(z * 2 + rr, kk * 2 + core)

    each(1, nz, lambda j: greet(ztok(z + j, r), c))
    each(1, chips, greet_chip)
    greet(tok, c + 1 - 2 * core)
    greet(z * 2 + 1 - r, c + 1 - 2 * core)
    pl.semaphore_wait(barrier, (nz - 1) + (chips - 1) + 2)

    partner = z * 2 + 1 - r
    sibling = c + 1 - 2 * core
    mine = pl.ds(pl.multiple_of(r * CH, CH), CH)
    other = pl.ds(pl.multiple_of((1 - r) * CH, CH), CH)

    swap_w = remote(w.at[:, other], wg.at[z, r], slot("w", 1), partner, c)
    swap_g = remote(cot.at[:, other], g.at[r], slot("g", 1), partner, c)
    swap_b = remote(b_in.at[k], bs.at[r], slot("b", 1), partner, c)
    swap_c = remote(c_in.at[k], cs.at[r], slot("c", 1), partner, c)
    swap_r = remote(raw_in, raw.at[r], slot("r", 1), partner, c)
    for swap in (swap_r, swap_g, swap_c, swap_b, swap_w):
        swap.start()

    ring_w = Ring("ring_w", wg)
    wg[z, r] = w[:, mine]
    ring_w.begin(r)

    def feat_out(j, s):
        rr, kk = chip(j)
        return remote(tokens, feat.at[c, r], s, z * 2 + rr, kk * 2 + core)

    def feat_on(j, s):
        rr, kk = chip(j)
        at = feat.at[kk * 2 + core, rr]
        return remote(at, at, s, tok, sibling)

    feats = Family("feats", 1, chips, feat_out)
    feats_on = Family("feats_on", 0, chips, feat_on)
    feat[c, r] = tokens[...]
    feats.start()
    feats_on.start_one(0)

    g[r] = cot[:, mine]
    bs[r] = b_in[k]
    cs[r] = c_in[k]
    raw[r] = raw_in[...]
    swap_w.wait_recv()
    ring_w.begin(1 - r)
    for swap in (swap_r, swap_g, swap_c, swap_b):
        swap.wait_recv()

    low_half = r == 0
    rows = []
    for p in range(2):
        both = raw[p]
        rows.append(jnp.where(low_half, both[0:HALF], both[HALF : 2 * HALF]))
    raw8 = jnp.concatenate(rows, axis=0)
    steps = jnp.maximum(raw8, 0.0) + jnp.log1p(jnp.exp(-jnp.abs(raw8)))
    for i in range(HALF):
        rate = jnp.full((1, TOK), rate_log[0, r * HALF + i], F32)
        skip = jnp.full((1, TOK), skip_in[0, r * HALF + i], F32)
        for p in range(2):
            vecs[0, p * HALF + i : p * HALF + i + 1, :] = rate
            vecs[1, p * HALF + i : p * HALF + i + 1, :] = skip
    rates = -jnp.exp(vecs[0])
    skips = vecs[1]
    ids0 = lax.broadcasted_iota(jnp.int32, (TOK, TOK), 0)
    ids1 = lax.broadcasted_iota(jnp.int32, (TOK, TOK), 1)
    upto = (ids0 <= ids1).astype(F32)
    log_decay = dot_exact(steps * rates, upto)
    log_total = jnp.broadcast_to(log_decay[:, TOK - 1 : TOK], (2 * HALF, TOK))
    start_decay = jnp.exp(log_decay)
    end_decay = jnp.exp(log_total - log_decay)
    end_weight = end_decay * steps
    block_decay = jnp.exp(log_total)
    decay_rows = [heads_to_rows(block_decay, p) for p in range(2)]
    columns = jnp.concatenate([log_decay, jnp.zeros((TOK - 2 * HALF, TOK), F32)], axis=0).T
    dtile[...] = jnp.concatenate(
        [block_decay[0:HALF] * block_decay[HALF : 2 * HALF], jnp.zeros((HALF, TOK), F32)], axis=0
    )
    dall[z] = dtile[...]

    def decay_out(j, s):
        return remote(dtile, dall.at[z], s, ztok(z + j, r), c)

    decays = Family("decays", 1, nz, decay_out)
    decays.start()

    adjoint = []
    for p in range(2):
        gt = g[p].astype(F32).T
        gtb[p] = gt.astype(BF16)
        gte[p] = gt * heads_to_rows(start_decay, p)
        adjoint.append(dot2(gte[p], cs[p]))
    a_last[...] = adjoint[1]

    def all_to_all(name, slot_of, whole):
        send_state[slot_of] = whole.astype(BF16).reshape(nz, piece, STATE)
        recv_state[slot_of, z] = send_state[slot_of, z]

        def out(j, s):
            to = lax.rem(z + j, nz)
            return remote(
                send_state.at[slot_of, to], recv_state.at[slot_of, z], s, ztok(to, r), c
            )

        first = Family(name + "_out", 1, nz, out)
        first.start()
        return first

    def prefix(name, slot_of, target, reverse):
        head = (z * piece) // HEAD

        def hop(n, carry):
            at = nz - 1 - n if reverse else n
            back_state[slot_of, at] = carry
            return dall[at, pl.ds(head, 1), :] * carry + recv_state[slot_of, at].astype(F32)

        lax.fori_loop(0, nz, hop, jnp.zeros((piece, STATE), F32))
        target[z] = back_state[slot_of, z]

        def back(j, s):
            to = lax.rem(z + j, nz)
            return remote(back_state.at[slot_of, to], target.at[z], s, ztok(to, r), c)

        second = Family(name + "_back", 1, nz, back)
        second.start()
        return second

    adj_out = all_to_all("adj", 0, adjoint[0] + decay_rows[0] * adjoint[1])
    ring_w.both(1)

    lower = ids0 >= ids1

    def block_kernels(p):
        inter[p] = dot(cs[p], bs[p], NT)
        for i in range(HALF):
            q = p * HALF + i
            gap = columns[:, q : q + 1] - log_decay[q : q + 1, :]
            dec[q] = jnp.where(lower, jnp.exp(jnp.minimum(gap, 0.0)), 0.0)
            kern = (dec[q] * inter[p]).astype(BF16)
            back_local[p, i * HEAD : (i + 1) * HEAD, :] = dot(
                gtb[p, i * HEAD : (i + 1) * HEAD, :], kern
            )

    block_kernels(0)
    ring_w.both(2)
    block_kernels(1)
    ring_w.both(3)
    decays.recv()
    adj_out.recv()
    adj_back = prefix("adj", 0, adj_in, True)
    ring_w.both(4)
    feats.recv()
    each(1, chips, feats_on.start_one)
    if nz // 2 > 5:
        ring_w.both(5)

    def column_out(j, s):
        to = lax.rem(z + j, nz)
        src = feat.at[
            to,
            r,
            pl.ds(pl.multiple_of(k * rowt, rowt), rowt),
            pl.ds(pl.multiple_of(core * TOK, TOK), TOK),
        ]
        return remote(src, tcol.at[r, k, core, z], s, ztok(to, r), c)

    feats_on.recv()
    own_columns = pltpu.make_async_copy(
        feat.at[
            z,
            r,
            pl.ds(pl.multiple_of(k * rowt, rowt), rowt),
            pl.ds(pl.multiple_of(core * TOK, TOK), TOK),
        ],
        tcol.at[r, k, core, z],
        local_sem.at[0],
    )
    own_columns.start()
    columns_out = Family("columns", 1, nz, column_out)
    columns_out.start()

    adj_back.recv()
    ring_i = Ring("ring_i", ig)
    late = adj_in[...].reshape(CH, STATE)
    adjoint_at = [decay_rows[1] * late + a_last[...], late]
    for p in range(2):
        abt[p] = dot2(adjoint_at[p], bs[p], NT)
        back = back_local[p] + heads_to_rows(end_decay, p) * abt[p]
        grad = heads_to_rows(skips, p) * gtb[p].astype(F32) + heads_to_rows(steps, p) * back
        grad_low = grad.astype(BF16)
        ig[z, p] = grad_low
        ring_i.begin(p)
        igtm[p * TOK : (p + 1) * TOK, :] = grad_low.astype(F32).T.astype(BF16)
    for s in range(6, nz // 2 + 1):
        ring_w.both(s)
    ring_i.both(1)

    def project(n, total):
        f = feat[n].reshape(2 * TOK, CH)
        return total + dot(f, wg[n].reshape(CH, CH))

    inputs = lax.fori_loop(0, nz, project, jnp.zeros((2 * TOK, CH), F32))
    states = []
    for p in range(2):
        xt = inputs[p * TOK : (p + 1) * TOK, :].astype(BF16).astype(F32).T
        xtb[p] = xt.astype(BF16)
        states.append(dot2(xt * heads_to_rows(end_weight, p), bs[p]))
    s_first[...] = states[0]
    state_out = all_to_all("state", 1, decay_rows[1] * states[0] + states[1])

    own_columns.wait()
    columns_out.recv()

    def tcol_out(j, s):
        rr, kk = chip(j)
        at = tcol.at[r, k, core]
        return remote(at, at, s, z * 2 + rr, kk * 2 + core)

    def tcol_on(j, s):
        rr, kk = chip(j)
        at = tcol.at[rr, kk, core]
        return remote(at, at, s, tok, sibling)

    tcols = Family("tcols", 1, chips, tcol_out)
    tcols_on = Family("tcols_on", 0, chips, tcol_on)
    tcols.start()
    tcols_on.start_one(0)
    if nz // 2 > 2:
        ring_i.both(2)

    def term(kk, side):
        n = kk * 2 + side
        out = dot(igtm[...], wg[n].reshape(CH, CH), NT)
        y_all[side, kk] = out.astype(BF16).reshape(2, TOK, CH)

    def y_to_sibling(j, s):
        return remote(y_all.at[1 - core, j], y_sib.at[j], s, tok, sibling)

    y_sibs = Family("y_sib", 0, nk, y_to_sibling)

    def first_terms(j):
        term(j, 1 - core)
        y_sibs.start_one(j)

    each(0, nk, first_terms)
    if nz // 2 > 3:
        ring_i.both(3)
    each(0, nk, lambda j: term(j, core))

    state_out.recv()
    state_back = prefix("state", 1, state_in, False)

    def y_sum(j):
        y_sibs.recv_one(j)
        y_out[j] = (y_all[core, j].astype(F32) + y_sib[j].astype(F32)).astype(BF16)

    each(0, nk, y_sum)
    y_in[0] = y_out[k, r]

    def y_chip(j, s):
        rr, kk = chip(j)
        return remote(y_out.at[kk, rr], y_in.at[j], s, z * 2 + rr, kk * 2 + core)

    y_outs = Family("y_out", 1, chips, y_chip)
    y_outs.start()
    if nz // 2 > 4:
        ring_i.both(4)

    rowsums = jnp.zeros((TOK, TOK), F32)
    colsums, ends, maps = [], [], []
    for p in range(2):
        pair_sum = jnp.zeros((TOK, TOK), F32)
        for i in range(HALF):
            q = p * HALF + i
            span = slice(i * HEAD, (i + 1) * HEAD)
            cross = dot(g[p, :, span], xtb[p, span, :])
            weights = dec[q] * cross
            pair_sum = pair_sum + weights * steps[q : q + 1, :]
            both = weights * inter[p]
            colsums.append(jnp.sum(both, axis=0, keepdims=True))
            row = jnp.sum(both * steps[q : q + 1, :], axis=1, keepdims=True)
            rowsums = jnp.where(ids1 == q, jnp.broadcast_to(row, (TOK, TOK)), rowsums)
            ends.append(
                jnp.sum(xtb[p, span, :].astype(F32) * abt[p, span, :], axis=0, keepdims=True)
            )
        maps.append(dot2(pair_sum, bs[p]))
        if nz // 2 > 5 + p:
            ring_i.both(5 + p)
    rowsums = rowsums.T[0 : 2 * HALF]

    state_back.recv()
    early = state_in[...].reshape(CH, STATE)
    state_at = [early, decay_rows[0] * early + s_first[...]]
    starts, corners = [], []
    for p in range(2):
        at_c = dot2(state_at[p], cs[p], NT)
        gs = gte[p]
        maps[p] = maps[p] + dot2(gs.T, state_at[p].astype(BF16))
        meets = adjoint_at[p] * state_at[p]
        for i in range(HALF):
            span = slice(i * HEAD, (i + 1) * HEAD)
            starts.append(jnp.sum(gs[span] * at_c[span], axis=0, keepdims=True))
            lanes = jnp.sum(meets[span], axis=0, keepdims=True)
            corners.append(
                jnp.broadcast_to(jnp.sum(lanes, axis=1, keepdims=True), (1, TOK))
            )
        m_own[p] = maps[p].reshape(2, TOK // 2, STATE)

    def map_to(j, s):
        rr, cc = (r + j // 2) % 2, (core + j % 2) % 2
        return remote(m_own.at[rr, cc], m_in.at[j], s, z * 2 + rr, 2 * k + cc)

    map_parts = Family("map_parts", 1, 4, map_to)
    map_parts.start()

    for n, parts in enumerate((colsums, ends, starts, corners)):
        for q in range(2 * HALF):
            vecs[2 + n, q : q + 1, :] = parts[q]
    colsum, end, start, corner = vecs[2], vecs[3], vecs[4], vecs[5]
    input_term = colsum + end_decay * end
    onward = (ids0 >= ids1).astype(F32)
    before = (ids0 < ids1).astype(F32)
    decay_term = (
        dot_exact(rowsums + start - steps * colsum, onward)
        + dot_exact(end_weight * end, before)
        + block_decay * corner
    )
    sigmoid = 1.0 / (1.0 + jnp.exp(-raw8))
    grads = sigmoid * (input_term + rates * decay_term)
    s_out[0, 0:HALF, :] = grads[0:HALF]
    s_out[0, HALF : 2 * HALF, :] = grads[0:HALF]
    s_out[1, 0:HALF, :] = grads[HALF : 2 * HALF]
    s_out[1, HALF : 2 * HALF, :] = grads[HALF : 2 * HALF]
    swap_s = remote(s_out.at[1 - r], s_swap, slot("s", 1), partner, c)
    swap_s.start()

    if nz // 2 > 7:
        ring_i.both(7)
    tcols.recv()
    each(1, chips, tcols_on.start_one)
    map_parts.recv()
    m_groups[k, core] = (m_own[r, core] + m_in[1] + m_in[2] + m_in[3]).astype(BF16)

    def map_out(j, s):
        at = m_groups.at[k, core]
        return remote(at, at, s, tok, xor(k, j, nk) * 2 + core)

    def map_on(j, s):
        at = m_groups.at[xor(k, j, nk), core]
        return remote(at, at, s, tok, sibling)

    map_outs = Family("map_out", 1, nk, map_out)
    map_ons = Family("map_on", 0, nk, map_on)
    map_outs.start()
    map_ons.start_one(0)
    ring_i.both(nz // 2)

    y_outs.recv()
    token_grad[...] = lax.fori_loop(
        0, chips, lambda j, total: total + y_in[j].astype(F32), jnp.zeros((TOK, CH), F32)
    ).astype(BF16)

    tcols_on.recv()

    def gather_term(n, totals):
        grad = ig[n]
        out = []
        for half in range(2):
            total = totals[half]
            for p in range(2):
                cols = tcol[p, :, half, n].reshape(TOK, TOK)
                total = total + dot(grad[p], cols)
            out.append(total)
        return tuple(out)

    zero = jnp.zeros((CH, TOK), F32)
    totals = lax.fori_loop(0, nz, gather_term, (zero, zero))
    for half in range(2):
        wgrad[half] = totals[half].T.astype(BF16)
    swap_o = remote(wgrad.at[1 - r], weight_grad.at[:, mine], slot("o", 1), partner, c)
    swap_o.start()
    weight_grad[:, mine] = wgrad[r]

    map_outs.recv()
    each(1, nk, map_ons.start_one)
    swap_s.wait_recv()
    own = jnp.where(low_half, s_out[0], s_out[1])
    sub = lax.broadcasted_iota(jnp.int32, (2 * HALF, TOK), 0)
    step_grad[...] = jnp.where((sub < HALF) == low_half, own, s_swap[...])
    map_ons.recv()
    for gg in range(nk):
        map_grad[gg] = m_groups[gg].reshape(TOK, STATE).astype(F32)
    swap_o.wait_recv()

    for swap in (swap_r, swap_g, swap_c, swap_b, swap_w, swap_s, swap_o):
        swap.wait_send()
    ring_w.sent()
    ring_i.sent()
    for family in (
        feats,
        feats_on,
        decays,
        adj_out,
        adj_back,
        state_out,
        state_back,
        columns_out,
        tcols,
        tcols_on,
        y_sibs,
        y_outs,
        map_parts,
        map_outs,
        map_ons,
    ):
        family.sent()


def local(tokens, w, cot, b, c, raw, rate_log, skip):
    nz = lax.axis_size("tok") // 2
    nk = lax.axis_size("ch") // 2
    piece, rowt, chips = CH // nz, TOK // nk, 2 * nk
    sems = 7 + 8 * (nz // 2 + 1) + 6 * nz + 6 * chips + 4 + 3 * nk
    vmem = pl.BlockSpec(memory_space=pltpu.VMEM)
    smem = pl.BlockSpec(memory_space=pltpu.SMEM)
    v = pltpu.VMEM

    def body(*refs):
        kernel(nz, nk, *refs)

    return pl.pallas_call(
        body,
        out_shape=(
            jax.ShapeDtypeStruct((TOK, CH), BF16),
            jax.ShapeDtypeStruct((TOK, 2 * CH), BF16),
            jax.ShapeDtypeStruct((2 * HALF, TOK), F32),
            jax.ShapeDtypeStruct((nk, TOK, STATE), F32),
        ),
        in_specs=[vmem] * 6 + [smem] * 2,
        out_specs=(vmem,) * 4,
        scratch_shapes=[
            v((2 * nk, 2, TOK, CH), BF16),
            v((nz, 2, TOK, CH), BF16),
            v((nz, 2, CH, TOK), BF16),
            v((2, nk, 2, nz, rowt, TOK), BF16),
            v((2, TOK, CH), BF16),
            v((2, TOK, STATE), BF16),
            v((2, TOK, STATE), BF16),
            v((2, 2 * HALF, TOK), F32),
            v((2 * HALF, TOK), F32),
            v((nz, 2 * HALF, TOK), F32),
            v((2, nz, piece, STATE), BF16),
            v((2, nz, piece, STATE), BF16),
            v((2, nz, piece, STATE), F32),
            v((nz, piece, STATE), F32),
            v((nz, piece, STATE), F32),
            v((2, CH, TOK), F32),
            v((2, CH, TOK), BF16),
            v((2, CH, TOK), BF16),
            v((2 * HALF, TOK, TOK), F32),
            v((2, TOK, TOK), F32),
            v((2, CH, TOK), F32),
            v((2, CH, TOK), F32),
            v((CH, STATE), F32),
            v((CH, STATE), F32),
            v((6, 2 * HALF, TOK), F32),
            v((2 * TOK, CH), BF16),
            v((2, nk, 2, TOK, CH), BF16),
            v((nk, 2, TOK, CH), BF16),
            v((nk, 2, TOK, CH), BF16),
            v((chips, TOK, CH), BF16),
            v((2, 2, TOK // 2, STATE), F32),
            v((4, TOK // 2, STATE), F32),
            v((nk, 2, TOK // 2, STATE), BF16),
            v((2, 2 * HALF, TOK), F32),
            v((2 * HALF, TOK), F32),
            v((2, TOK, CH), BF16),
            pltpu.SemaphoreType.DMA((1,)),
            pltpu.SemaphoreType.DMA((sems,)),
            pltpu.SemaphoreType.DMA((sems,)),
        ],
        compiler_params=pltpu.CompilerParams(
            collective_id=0, has_side_effects=True, vmem_limit_bytes=48 * 1024 * 1024
        ),
        name="mixer_backward",
    )(tokens, w, cot, b, c, raw, rate_log.reshape(1, 2 * HALF), skip.reshape(1, 2 * HALF))


def solution(mesh):
    return jax.shard_map(
        local,
        mesh=mesh,
        in_specs=(
            P("tok", "ch"),
            P("tok", "ch"),
            P("tok", "ch"),
            P(None, "tok", None),
            P(None, "tok", None),
            P("ch", "tok"),
            P("ch"),
            P("ch"),
        ),
        out_specs=(P("tok", "ch"), P("tok", "ch"), P("ch", "tok"), P(None, "tok", None)),
        check_vma=False,
    )
```

time: 935 us -> 122 us (0.13)
  waiting for transfers between devices: 734 us -> 0 us
  Pallas kernels: 0 us -> 112 us
  blocking collectives: 70.8 us -> 0 us
  other arithmetic: 68.6 us -> 0 us
  matrix products: 26 us -> 0 us
  between operations: 15 us -> 0.67 us
    all_gather x5 -> x0, waiting for transfers between devices: 533 us -> none  [the longest x2 281 us: prefix(): lax.all_gather(part.astype(kind), axis)]
    psum x1 -> x0, waiting for transfers between devices: 131 us -> none  [local(): lax.psum(map_terms.astype(jnp.bfloat16), 'ch').astype(jnp.float32)]
    pallas_call x0 -> x1, Pallas kernels: none -> 112 us  [local(): pl.pallas_call(body, out_shape=(jax.ShapeDtypeStruct((TOK, CH), BF16), ja...]
    unnamed x1 -> x0, blocking collectives: 70.8 us -> none
    reduce_scatter x1 -> x0, waiting for transfers between devices: 69.7 us -> none  [local(): lax.psum_scatter(partial_grad.astype(jnp.bfloat16), 'ch', scatter_dimensi...]
    select_n x65 -> x0, other arithmetic: 64.9 us -> none  [the longest x64 64.9 us: hop(): return jax.tree.map(lambda a, b: jnp.where(reached, a, b), new, before)]
    dot_general x18 -> x0, matrix products: 26 us -> none  [the longest x1 4.75 us: local(): lax.dot_general(input_grad, lax.all_gather(w_input, 'tok', axis=0, tiled=...]
  transfers between devices with their start and end apart: 8 -> 0, of which waited for: 6 -> 0; matrix products, arithmetic and copies ran while one was open for 11% -> 0% of each run, Pallas kernels for 0% -> 0%
where the time goes in v1:
time: 122 us; the launch traced here: 121 us
  Pallas kernels  112 us (92%)
  local copies, waits for them, and re-layouts  8.56 us (7%)
    pallas_call x1, Pallas kernels, local(): pl.pallas_call(body, out_shape=(jax.ShapeDtypeStruct((TOK, CH), BF16), ja...  112 us
    unnamed x20, local copies, waits for them, and re-layouts  8.56 us

profile of v1, /device:TPU:1, one launch (start us, length us, event | category | flops | bytes accessed | tf_op | source)
XLA Modules:
  0.0 121.5 jit_solution(13022498291821776349)
XLA Ops:
  0.6 0.0 copy-start.6
  0.6 0.0 copy-start.7
  0.7 0.6 copy-done.6
  1.3 0.0 copy-done.7
  1.3 0.0 copy-start
  1.3 0.9 copy-done
  2.3 0.0 copy-start.1
  2.3 0.9 copy-done.1
  3.2 0.0 copy-start.2
  3.2 0.9 copy-done.2
  4.1 0.0 copy-start.3
  4.1 0.9 copy-done.3
  5.0 0.0 copy-start.4
  5.0 0.8 copy-done.4
  5.9 0.0 copy-start.5
  5.9 0.7 copy-done.5
  6.5 112.2 %mixer_backward.1 = (bf16[128,256]{1,0:T(8,128)(2,1)S(1)}, bf16[128,512]{1,0:T(8,128)(2,1)S(1)}, f32[8,128]{1,0:T(8,128)S(1)}, f32[8,128,128]{2,1,0:T(8,128)S(1)}) custom-call(bf16[128,256]{1,0:T(8,128)(2,1)S(1)} %copy-done.4, bf16[128,512]{1,0:T(8,128)(2,1)S(1)} %copy-done.2, bf16[128,512]{1,0:T(8,128)(2,1)S(1)} %copy-done.3, ...), custom_call_target="tpu_custom_call" | custom-call | tf_op jit(solution)/shard_map/mixer_backward/pallas_call | solution.py:643
  118.8 0.6 copy.16
  119.4 0.7 copy.17
  120.1 0.6 copy.18
  120.7 0.8 copy.19
Async XLA Ops:
  0.6 0.7 copy-start.6
  0.6 0.7 copy-start.7
  1.3 0.9 copy-start
  2.3 0.9 copy-start.1
  3.2 0.9 copy-start.2
  4.1 0.9 copy-start.3
  5.0 0.8 copy-start.4
  5.9 0.7 copy-start.5

commit v2 on v1

v2 whole, which is shorter than its diff:
```python
import jax
import jax.numpy as jnp
from jax import lax
from jax.experimental import pallas as pl
from jax.experimental.pallas import tpu as pltpu
from jax.sharding import PartitionSpec as P

MESH = pl.DeviceIdType.MESH
HIGHEST = lax.Precision.HIGHEST
F32 = jnp.float32
BF16 = jnp.bfloat16
TOK = 128
HEAD = 64
HALF = 4
CH = HALF * HEAD
STATE = 128

NN = (((1,), (0,)), ((), ()))
NT = (((1,), (1,)), ((), ()))


def dot(a, b, dims=NN):
    return lax.dot_general(a, b, dims, preferred_element_type=F32)


def dot2(a, b, dims=NN):
    high = a.astype(BF16)
    low = (a - high.astype(F32)).astype(BF16)
    return dot(high, b, dims) + dot(low, b, dims)


def dot_exact(a, b):
    return lax.dot_general(a, b, NN, precision=HIGHEST, preferred_element_type=F32)


def heads_to_rows(rows, p):
    return jnp.concatenate(
        [
            jnp.broadcast_to(rows[p * HALF + i : p * HALF + i + 1], (HEAD, rows.shape[1]))
            for i in range(HALF)
        ],
        axis=0,
    )


def kernel(
    nz,
    nk,
    tokens,
    w,
    cot,
    b_in,
    c_in,
    raw_in,
    rate_log,
    skip_in,
    token_grad,
    weight_grad,
    step_grad,
    map_grad,
    feat,
    wg,
    ig,
    tcol,
    w_other,
    cot_other,
    b_other,
    c_other,
    raw_own,
    g,
    bs,
    cs,
    raw,
    dtile,
    dall,
    send_state,
    recv_state,
    back_state,
    state_in,
    gte,
    gtb,
    xtb,
    dec,
    inter,
    back_local,
    abt,
    a_last,
    s_first,
    vecs,
    igtm,
    proj,
    wtot,
    y_all,
    y_sib,
    y_out,
    y_in,
    m_own,
    m_in,
    m_groups,
    s_out,
    s_swap,
    wgrad,
    local_sem,
    send_sem,
    recv_sem,
):
    tok, c = lax.axis_index("tok"), lax.axis_index("ch")
    z, r = tok // 2, tok % 2
    k, core = c // 2, c % 2
    piece = CH // nz
    rowt = TOK // nk
    chips = 2 * nk
    hops = nz // 2
    partner = z * 2 + 1 - r
    sibling = c + 1 - 2 * core
    across = lax.rem(k + nk // 2, nk)
    mine = pl.ds(pl.multiple_of(r * CH, CH), CH)
    other = pl.ds(pl.multiple_of((1 - r) * CH, CH), CH)

    def ztok(zz, rr):
        return lax.rem(zz + nz, nz) * 2 + rr

    def xor(a, b, n):
        out, bit = 0, 1
        while bit < n:
            pa, pb = (a // bit) % 2, (b // bit) % 2
            out = out + bit * ((pa + pb) % 2)
            bit *= 2
        return out

    def chip(j):
        return (r + j // nk) % 2, xor(k, j % nk, nk)

    sends, recvs = [0], [0]

    def take(counter, n=1):
        counter[0] += n
        return counter[0] - n

    def remote(src, dst, s, q, tok_to, ch_to):
        return pltpu.make_async_remote_copy(
            src_ref=src,
            dst_ref=dst,
            send_sem=send_sem.at[s],
            recv_sem=recv_sem.at[q],
            device_id=(tok_to, ch_to),
            device_id_type=MESH,
        )

    def single(src, dst, tok_to, ch_to):
        return remote(src, dst, take(sends), take(recvs), tok_to, ch_to)

    def each(first, last, f):
        def body(j, carry):
            f(j)
            return carry

        lax.fori_loop(first, last, body, 0)

    class Family:
        def __init__(self, first, last, make, whole):
            self.first, self.last, self.whole = first, last, whole
            self.s, self.q = take(sends), take(recvs)
            self.make = lambda j: remote(*make(j)[:2], self.s, self.q, *make(j)[2:])
            self.all = lambda: remote(whole, whole, self.s, self.q, tok, sibling)

        def start(self):
            each(self.first, self.last, lambda j: self.make(j).start())

        def start_one(self, j):
            self.make(j).start()

        def recv(self):
            self.all().wait_recv()

        def sent(self):
            self.all().wait_send()

    class Ring:
        def __init__(self, buf, first):
            self.buf, self.first = buf, first
            self.rows = buf.shape[2] // 2
            self.s, self.q = take(sends), take(recvs, 8 * (hops + 1))

        def copy(self, way, s, n):
            block = lax.rem(z - way * (s - 1) + 2 * nz, nz)
            side = lax.rem(self.first + n // 2, 2)
            at = self.buf.at[block, side, pl.ds((n % 2) * self.rows, self.rows)]
            q = self.q + (s * 2 + (0 if way == 1 else 1)) * 4 + n
            return remote(at, at, self.s, q, ztok(z + way, r), c)

        def has(self, way, s, n):
            if s < hops:
                return True
            return s == hops and (n < 2) == (way == 1)

        def begin(self, n):
            for way in (1, -1):
                self.copy(way, 1, n).start()

        def tick(self, s, n):
            for way in (1, -1):
                if self.has(way, s, n):
                    self.copy(way, s, n).wait_recv()
                    if self.has(way, s + 1, n):
                        self.copy(way, s + 1, n).start()

        def ticks(self, group):
            for s, n in group:
                self.tick(s, n)

        def sent(self):
            whole = self.buf.at[pl.ds(0, nz - 1)]
            remote(whole, whole, self.s, self.q, tok, sibling).wait_send()

    loads = [
        pltpu.make_async_copy(src, dst, local_sem.at[n])
        for n, (src, dst) in enumerate(
            (
                (raw_in, raw_own),
                (cot.at[:, other], cot_other),
                (c_in.at[across], c_other),
                (w.at[:, mine], wg.at[z, r]),
                (w.at[:, other], w_other),
                (b_in.at[across], b_other),
                (tokens, feat.at[c, r]),
                (cot.at[:, mine], g.at[r]),
                (c_in.at[k], cs.at[r]),
                (b_in.at[k], bs.at[r]),
            )
        )
    ]
    for load in loads:
        load.start()

    barrier = pltpu.get_barrier_semaphore()

    def greet(tok_to, ch_to):
        pl.semaphore_signal(barrier, inc=1, device_id=(tok_to, ch_to), device_id_type=MESH)

    def greet_chip(j):
        rr, kk = chip(j)
        greet(z * 2 + rr, kk * 2 + core)

    each(1, nz, lambda j: greet(ztok(z + j, r), c))
    each(1, chips, greet_chip)
    greet(tok, sibling)
    greet(partner, sibling)
    for load in loads:
        load.wait()
    pl.semaphore_wait(barrier, (nz - 1) + (chips - 1) + 2)

    ring_w = Ring(wg, r)
    swap_r = single(raw_own, raw.at[r], partner, c)
    swap_g = single(cot_other, g.at[r], partner, c)
    swap_c = single(c_other, cs.at[r], partner, across * 2 + core)
    swap_w = single(w_other, wg.at[z, r], partner, c)
    swap_b = single(b_other, bs.at[r], partner, across * 2 + core)
    swap_r.start()
    swap_g.start()
    swap_c.start()
    ring_w.begin(0)
    ring_w.begin(1)
    swap_w.start()
    swap_b.start()

    def feat_out(j):
        rr, kk = chip(j)
        at = feat.at[c, r]
        return at, at, z * 2 + rr, kk * 2 + core

    def feat_on(j):
        rr, kk = chip(j)
        at = feat.at[kk * 2 + core, rr]
        return at, at, tok, sibling

    feats = Family(1, chips, feat_out, feat.at[pl.ds(0, chips - 1), 0])
    feats_on = Family(0, chips, feat_on, feat.at[:, 0])
    feats.start()
    feats_on.start_one(0)
    raw[r] = raw_own[...]

    groups_w = []
    for t in range(1, hops + 3):
        group = [(t, 0), (t, 1)] if t <= hops else []
        groups_w.append(group + ([(t - 2, 2), (t - 2, 3)] if t > 2 else []))
    groups_w += [[]] * (10 - len(groups_w))
    groups_i = [[(s, n) for n in range(4)] for s in range(1, hops)]
    groups_i += [[]] * (7 - len(groups_i)) + [[(hops, n) for n in range(4)]]

    ring_w.ticks(groups_w[0])
    swap_r.wait_recv()

    low_half = r == 0
    rows = []
    for p in range(2):
        both = raw[p]
        rows.append(jnp.where(low_half, both[0:HALF], both[HALF : 2 * HALF]))
    raw8 = jnp.concatenate(rows, axis=0)
    steps = jnp.maximum(raw8, 0.0) + jnp.log1p(jnp.exp(-jnp.abs(raw8)))
    for i in range(HALF):
        rate = jnp.full((1, TOK), rate_log[0, r * HALF + i], F32)
        skip = jnp.full((1, TOK), skip_in[0, r * HALF + i], F32)
        for p in range(2):
            vecs[0, p * HALF + i : p * HALF + i + 1, :] = rate
            vecs[1, p * HALF + i : p * HALF + i + 1, :] = skip
    rates = -jnp.exp(vecs[0])
    skips = vecs[1]
    ids0 = lax.broadcasted_iota(jnp.int32, (TOK, TOK), 0)
    ids1 = lax.broadcasted_iota(jnp.int32, (TOK, TOK), 1)
    upto = (ids0 <= ids1).astype(F32)
    log_decay = dot_exact(steps * rates, upto)
    log_total = jnp.broadcast_to(log_decay[:, TOK - 1 : TOK], (2 * HALF, TOK))
    start_decay = jnp.exp(log_decay)
    end_decay = jnp.exp(log_total - log_decay)
    end_weight = end_decay * steps
    block_decay = jnp.exp(log_total)
    decay_rows = [heads_to_rows(block_decay, p) for p in range(2)]
    columns = jnp.concatenate([log_decay, jnp.zeros((TOK - 2 * HALF, TOK), F32)], axis=0).T
    dtile[...] = jnp.concatenate(
        [block_decay[0:HALF] * block_decay[HALF : 2 * HALF], jnp.zeros((HALF, TOK), F32)], axis=0
    )
    dall[z] = dtile[...]

    def decay_out(j):
        return dtile, dall.at[z], ztok(z + j, r), c

    decays = Family(1, nz, decay_out, dall.at[pl.ds(0, nz - 1)])
    decays.start()
    ring_w.ticks(groups_w[1])

    swap_g.wait_recv()
    swap_c.wait_recv()
    adjoint = []
    for p in range(2):
        gt = g[p].astype(F32).T
        gtb[p] = gt.astype(BF16)
        gte[p] = gt * heads_to_rows(start_decay, p)
        adjoint.append(dot2(gte[p], cs[p]))
    a_last[...] = adjoint[1]

    class Exchange:
        def __init__(self, n, reverse):
            self.n, self.reverse = n, reverse

            def out(j):
                to = lax.rem(z + j, nz)
                return send_state.at[n, to], recv_state.at[n, z], ztok(to, r), c

            def back(j):
                to = lax.rem(z + j, nz)
                return back_state.at[n, to], state_in.at[n, z], ztok(to, r), c

            self.out = Family(1, nz, out, recv_state.at[n, pl.ds(0, nz - 1)])
            self.back = Family(1, nz, back, state_in.at[n, pl.ds(0, nz - 1)])

        def start(self, whole):
            n = self.n
            send_state[n] = whole.astype(BF16).reshape(nz, piece, STATE)
            self.out.start()
            recv_state[n, z] = send_state[n, z]

        def prefix(self):
            n = self.n
            head = (z * piece) // HEAD
            self.out.recv()
            carry = jnp.zeros((piece, STATE), F32)
            for at in reversed(range(nz)) if self.reverse else range(nz):
                back_state[n, at] = carry.astype(BF16)
                carry = dall[at, pl.ds(head, 1), :] * carry + recv_state[n, at].astype(F32)
            self.back.start()
            state_in[n, z] = back_state[n, z]

        def result(self):
            self.back.recv()
            return state_in[self.n].astype(F32).reshape(CH, STATE)

    adjoints = Exchange(0, True)
    adjoints.start(adjoint[0] + decay_rows[0] * adjoint[1])
    swap_w.wait_recv()
    ring_w.begin(2)
    ring_w.begin(3)
    ring_w.ticks(groups_w[2])
    swap_b.wait_recv()

    lower = ids0 >= ids1

    def block_kernels(p, heads):
        if heads[0] == 0:
            inter[p] = dot(cs[p], bs[p], NT)
        for i in heads:
            q = p * HALF + i
            gap = columns[:, q : q + 1] - log_decay[q : q + 1, :]
            dec[q] = jnp.where(lower, jnp.exp(jnp.minimum(gap, 0.0)), 0.0)
            kern = (dec[q] * inter[p]).astype(BF16)
            back_local[p, i * HEAD : (i + 1) * HEAD, :] = dot(
                gtb[p, i * HEAD : (i + 1) * HEAD, :], kern
            )

    block_kernels(0, (0, 1))
    ring_w.ticks(groups_w[3][:2])
    decays.recv()
    adjoints.prefix()
    ring_w.ticks(groups_w[3][2:])
    block_kernels(0, (2, 3))
    ring_w.ticks(groups_w[4][:2])
    block_kernels(1, (0, 1))
    ring_w.ticks(groups_w[4][2:])
    block_kernels(1, (2, 3))
    ring_w.ticks(groups_w[5])

    late = adjoints.result()
    ring_i = Ring(ig, 0)
    adjoint_at = [decay_rows[1] * late + a_last[...], late]
    for p in range(2):
        abt[p] = dot2(adjoint_at[p], bs[p], NT)
        back = back_local[p] + heads_to_rows(end_decay, p) * abt[p]
        grad = heads_to_rows(skips, p) * gtb[p].astype(F32) + heads_to_rows(steps, p) * back
        grad_low = grad.astype(BF16)
        ig[z, p] = grad_low
        ring_i.begin(2 * p)
        ring_i.begin(2 * p + 1)
        igtm[p * TOK : (p + 1) * TOK, :] = grad_low.astype(F32).T.astype(BF16)
    ring_w.ticks(groups_w[6])
    feats.recv()
    each(1, chips, feats_on.start_one)
    ring_i.ticks(groups_i[0])
    ring_w.ticks(groups_w[7])
    feats_on.recv()

    own_rows = pl.ds(pl.multiple_of(k * rowt, rowt), rowt)
    own_lanes = pl.ds(pl.multiple_of(core * TOK, TOK), TOK)
    me = r * nk + k

    def column_out(j):
        to = lax.rem(z + j, nz)
        src = feat.at[to, r, own_rows, own_lanes]
        return src, tcol.at[me, core, z], ztok(to, r), c

    own_columns = pltpu.make_async_copy(
        feat.at[z, r, own_rows, own_lanes], tcol.at[me, core, z], local_sem.at[0]
    )
    columns_out = Family(1, nz, column_out, tcol.at[0, 0, pl.ds(0, nz - 1)])

    def project(first, last):
        total = proj[...] if first else jnp.zeros((2 * TOK, CH), F32)
        for d in range(first, last):
            for way in (1, -1) if 0 < d < hops else (1,):
                n = lax.rem(z + way * d + nz, nz)
                total = total + dot(feat[n].reshape(2 * TOK, CH), wg[n].reshape(CH, CH))
        proj[...] = total

    project(0, min(3, hops))
    if hops > 3:
        ring_w.ticks(groups_w[8][:1])
        project(3, 6)
    ring_w.ticks(groups_w[8][1:] if hops > 3 else groups_w[8])
    ring_i.ticks(groups_i[1][:2])
    ring_w.ticks(groups_w[9])
    project(min(6, hops), hops + 1)
    states = []
    for p in range(2):
        xt = proj[p * TOK : (p + 1) * TOK, :].astype(BF16).astype(F32).T
        xtb[p] = xt.astype(BF16)
        states.append(dot2(xt * heads_to_rows(end_weight, p), bs[p]))
    s_first[...] = states[0]
    scan = Exchange(1, False)
    scan.start(decay_rows[1] * states[0] + states[1])
    own_columns.start()
    columns_out.start()
    ring_i.ticks(groups_i[1][2:])

    def term(kk, side):
        n = kk * 2 + side
        out = dot(igtm[...], wg[n].reshape(CH, CH), NT)
        y_all[side, kk] = out.astype(BF16).reshape(2, TOK, CH)

    def y_to_sibling(j):
        return y_all.at[1 - core, j], y_sib.at[j], tok, sibling

    y_sibs = Family(0, nk, y_to_sibling, y_sib)

    def first_terms(j):
        term(j, 1 - core)
        y_sibs.start_one(j)

    each(0, nk // 2, first_terms)
    ring_i.ticks(groups_i[2][:2])
    each(nk // 2, nk, first_terms)
    ring_i.ticks(groups_i[2][2:])

    scan.prefix()
    own_columns.wait()
    columns_out.recv()

    def tcol_out(j):
        rr, kk = chip(j)
        at = tcol.at[me, core]
        return at, at, z * 2 + rr, kk * 2 + core

    def tcol_on(j):
        rr, kk = chip(j)
        at = tcol.at[rr * nk + kk, core]
        return at, at, tok, sibling

    tcols = Family(1, chips, tcol_out, tcol.at[pl.ds(0, chips - 1), 0])
    tcols_on = Family(0, chips, tcol_on, tcol.at[:, 0])
    tcols.start()
    tcols_on.start_one(0)
    ring_i.ticks(groups_i[3][:2])
    each(0, nk // 2, lambda j: term(j, core))
    ring_i.ticks(groups_i[3][2:])
    each(nk // 2, nk, lambda j: term(j, core))

    rowsums = jnp.zeros((TOK, TOK), F32)
    colsums, ends, maps = [], [], []

    def pairs(p, heads, pair_sum, rowsums):
        for i in heads:
            q = p * HALF + i
            span = slice(i * HEAD, (i + 1) * HEAD)
            cross = dot(g[p, :, span], xtb[p, span, :])
            weights = dec[q] * cross
            pair_sum = pair_sum + weights * steps[q : q + 1, :]
            both = weights * inter[p]
            colsums.append(jnp.sum(both, axis=0, keepdims=True))
            row = jnp.sum(both * steps[q : q + 1, :], axis=1, keepdims=True)
            rowsums = jnp.where(ids1 == q, jnp.broadcast_to(row, (TOK, TOK)), rowsums)
            ends.append(
                jnp.sum(xtb[p, span, :].astype(F32) * abt[p, span, :], axis=0, keepdims=True)
            )
        return pair_sum, rowsums

    for p in range(2):
        pair_sum = jnp.zeros((TOK, TOK), F32)
        pair_sum, rowsums = pairs(p, (0, 1), pair_sum, rowsums)
        ring_i.ticks(groups_i[4][2 * p : 2 * p + 2])
        pair_sum, rowsums = pairs(p, (2, 3), pair_sum, rowsums)
        maps.append(dot2(pair_sum, bs[p]))
    rowsums = rowsums.T[0 : 2 * HALF]

    early = scan.result()
    state_at = [early, decay_rows[0] * early + s_first[...]]
    starts, corners = [], []
    for p in range(2):
        at_c = dot2(state_at[p], cs[p], NT)
        gs = gte[p]
        maps[p] = maps[p] + dot2(gs.T, state_at[p].astype(BF16))
        meets = adjoint_at[p] * state_at[p]
        for i in range(HALF):
            span = slice(i * HEAD, (i + 1) * HEAD)
            starts.append(jnp.sum(gs[span] * at_c[span], axis=0, keepdims=True))
            lanes = jnp.sum(meets[span], axis=0, keepdims=True)
            corners.append(
                jnp.broadcast_to(jnp.sum(lanes, axis=1, keepdims=True), (1, TOK))
            )
        m_own[p] = maps[p].reshape(2, TOK // 2, STATE)

    def map_to(j):
        rr, cc = (r + j // 2) % 2, (core + j % 2) % 2
        return m_own.at[rr, cc], m_in.at[j], z * 2 + rr, 2 * k + cc

    map_parts = Family(1, 4, map_to, m_in.at[pl.ds(1, 3)])
    map_parts.start()
    ring_i.ticks(groups_i[5])

    def y_sum(j):
        y_out[j] = (y_all[core, j].astype(F32) + y_sib[j].astype(F32)).astype(BF16)

    y_sibs.recv()
    each(0, nk, y_sum)
    y_in[0] = y_out[k, r]

    def y_chip(j):
        rr, kk = chip(j)
        return y_out.at[kk, rr], y_in.at[j], z * 2 + rr, kk * 2 + core

    y_outs = Family(1, chips, y_chip, y_in.at[pl.ds(1, chips - 1)])
    y_outs.start()

    for n, parts in enumerate((colsums, ends, starts, corners)):
        for q in range(2 * HALF):
            vecs[2 + n, q : q + 1, :] = parts[q]
    colsum, end, start, corner = vecs[2], vecs[3], vecs[4], vecs[5]
    input_term = colsum + end_decay * end
    onward = (ids0 >= ids1).astype(F32)
    before = (ids0 < ids1).astype(F32)
    decay_term = (
        dot_exact(rowsums + start - steps * colsum, onward)
        + dot_exact(end_weight * end, before)
        + block_decay * corner
    )
    sigmoid = 1.0 / (1.0 + jnp.exp(-raw8))
    grads = sigmoid * (input_term + rates * decay_term)
    s_out[0, 0:HALF, :] = grads[0:HALF]
    s_out[0, HALF : 2 * HALF, :] = grads[0:HALF]
    s_out[1, 0:HALF, :] = grads[HALF : 2 * HALF]
    s_out[1, HALF : 2 * HALF, :] = grads[HALF : 2 * HALF]
    swap_s = single(s_out.at[1 - r], s_swap, partner, c)
    swap_s.start()

    map_parts.recv()
    m_groups[k, core] = (m_own[r, core] + m_in[1] + m_in[2] + m_in[3]).astype(BF16)

    def map_out(j):
        at = m_groups.at[k, core]
        return at, at, tok, xor(k, j, nk) * 2 + core

    def map_on(j):
        at = m_groups.at[xor(k, j, nk), core]
        return at, at, tok, sibling

    map_outs = Family(1, nk, map_out, m_groups.at[pl.ds(0, nk - 1), 0])
    map_ons = Family(0, nk, map_on, m_groups.at[:, 0])
    map_outs.start()
    map_ons.start_one(0)
    ring_i.ticks(groups_i[6][:2])
    tcols.recv()
    each(1, chips, tcols_on.start_one)
    ring_i.ticks(groups_i[6][2:])

    def gather(first, last):
        for half in range(2):
            total = wtot[half] if first else jnp.zeros((CH, TOK), F32)
            for d in range(first, last):
                for way in (1, -1) if 0 < d < hops else (1,):
                    n = lax.rem(z + way * d + nz, nz)
                    for p in range(2):
                        cols = tcol[p * nk : (p + 1) * nk, half, n].reshape(TOK, TOK)
                        total = total + dot(ig[n, p], cols)
            wtot[half] = total

    swap_s.wait_recv()
    own = jnp.where(low_half, s_out[0], s_out[1])
    sub = lax.broadcasted_iota(jnp.int32, (2 * HALF, TOK), 0)
    step_grad[...] = jnp.where((sub < HALF) == low_half, own, s_swap[...])
    map_outs.recv()
    each(1, nk, map_ons.start_one)
    tcols_on.recv()
    gather(0, hops)
    ring_i.ticks(groups_i[7])
    gather(hops, hops + 1)
    for half in range(2):
        wgrad[half] = wtot[half].T.astype(BF16)
    swap_o = single(wgrad.at[1 - r], weight_grad.at[:, mine], partner, c)
    swap_o.start()
    weight_grad[:, mine] = wgrad[r]

    y_outs.recv()
    total = y_in[0].astype(F32)
    for j in range(1, chips):
        total = total + y_in[j].astype(F32)
    token_grad[...] = total.astype(BF16)
    map_ons.recv()
    for gg in range(nk):
        map_grad[gg] = m_groups[gg].reshape(TOK, STATE).astype(F32)

    for swap in (swap_r, swap_g, swap_c, swap_b, swap_w, swap_s):
        swap.wait_send()
    ring_w.sent()
    ring_i.sent()
    for family in (
        feats,
        feats_on,
        decays,
        adjoints.out,
        adjoints.back,
        scan.out,
        scan.back,
        columns_out,
        tcols,
        tcols_on,
        y_sibs,
        y_outs,
        map_parts,
        map_outs,
        map_ons,
    ):
        family.sent()
    swap_o.wait_recv()
    swap_o.wait_send()


def local(tokens, w, cot, b, c, raw, rate_log, skip):
    nz = lax.axis_size("tok") // 2
    nk = lax.axis_size("ch") // 2
    piece, rowt, chips = CH // nz, TOK // nk, 2 * nk
    vmem = pl.BlockSpec(memory_space=pltpu.VMEM)
    smem = pl.BlockSpec(memory_space=pltpu.SMEM)
    hbm = pl.BlockSpec(memory_space=pl.ANY)
    v = pltpu.VMEM

    def body(*refs):
        kernel(nz, nk, *refs)

    return pl.pallas_call(
        body,
        out_shape=(
            jax.ShapeDtypeStruct((TOK, CH), BF16),
            jax.ShapeDtypeStruct((TOK, 2 * CH), BF16),
            jax.ShapeDtypeStruct((2 * HALF, TOK), F32),
            jax.ShapeDtypeStruct((nk, TOK, STATE), F32),
        ),
        in_specs=[hbm] * 6 + [smem] * 2,
        out_specs=(vmem,) * 4,
        scratch_shapes=[
            v((2 * nk, 2, TOK, CH), BF16),
            v((nz, 2, TOK, CH), BF16),
            v((nz, 2, CH, TOK), BF16),
            v((2 * nk, 2, nz, rowt, TOK), BF16),
            v((TOK, CH), BF16),
            v((TOK, CH), BF16),
            v((TOK, STATE), BF16),
            v((TOK, STATE), BF16),
            v((2 * HALF, TOK), F32),
            v((2, TOK, CH), BF16),
            v((2, TOK, STATE), BF16),
            v((2, TOK, STATE), BF16),
            v((2, 2 * HALF, TOK), F32),
            v((2 * HALF, TOK), F32),
            v((nz, 2 * HALF, TOK), F32),
            v((2, nz, piece, STATE), BF16),
            v((2, nz, piece, STATE), BF16),
            v((2, nz, piece, STATE), BF16),
            v((2, nz, piece, STATE), BF16),
            v((2, CH, TOK), F32),
            v((2, CH, TOK), BF16),
            v((2, CH, TOK), BF16),
            v((2 * HALF, TOK, TOK), F32),
            v((2, TOK, TOK), F32),
            v((2, CH, TOK), F32),
            v((2, CH, TOK), F32),
            v((CH, STATE), F32),
            v((CH, STATE), F32),
            v((6, 2 * HALF, TOK), F32),
            v((2 * TOK, CH), BF16),
            v((2 * TOK, CH), F32),
            v((2, CH, TOK), F32),
            v((2, nk, 2, TOK, CH), BF16),
            v((nk, 2, TOK, CH), BF16),
            v((nk, 2, TOK, CH), BF16),
            v((chips, TOK, CH), BF16),
            v((2, 2, TOK // 2, STATE), F32),
            v((4, TOK // 2, STATE), F32),
            v((nk, 2, TOK // 2, STATE), BF16),
            v((2, 2 * HALF, TOK), F32),
            v((2 * HALF, TOK), F32),
            v((2, TOK, CH), BF16),
            pltpu.SemaphoreType.DMA((10,)),
            pltpu.SemaphoreType.DMA((24,)),
            pltpu.SemaphoreType.DMA((22 + 16 * (nz // 2 + 1),)),
        ],
        compiler_params=pltpu.CompilerParams(
            collective_id=0, has_side_effects=True, vmem_limit_bytes=60 * 1024 * 1024
        ),
        name="mixer_backward",
    )(tokens, w, cot, b, c, raw, rate_log.reshape(1, 2 * HALF), skip.reshape(1, 2 * HALF))


def solution(mesh):
    return jax.shard_map(
        local,
        mesh=mesh,
        in_specs=(
            P("tok", "ch"),
            P("tok", "ch"),
            P("tok", "ch"),
            P(None, "tok", None),
            P(None, "tok", None),
            P("ch", "tok"),
            P("ch"),
            P("ch"),
        ),
        out_specs=(P("tok", "ch"), P("tok", "ch"), P("ch", "tok"), P(None, "tok", None)),
        check_vma=False,
    )
```

time: 122 us -> 110 us (0.902); the launches traced: 121 us -> 108 us
  Pallas kernels: 112 us -> 102 us
  local copies, waits for them, and re-layouts: 8.56 us -> 4.65 us
    pallas_call x1, Pallas kernels: 112 us -> 102 us  [local(): pl.pallas_call(body, out_shape=(jax.ShapeDtypeStruct((TOK, CH), BF16), ja...]
    unnamed x20 -> x8, local copies, waits for them, and re-layouts: 8.56 us -> 4.65 us
where the time goes in v2:
time: 110 us; the launch traced here: 108 us
  Pallas kernels  102 us (93%)
  local copies, waits for them, and re-layouts  4.65 us (4%)
    pallas_call x1, Pallas kernels, local(): pl.pallas_call(body, out_shape=(jax.ShapeDtypeStruct((TOK, CH), BF16), ja...  102 us
    unnamed x8, local copies, waits for them, and re-layouts  4.65 us

profile of v2, /device:TPU:1, one launch (start us, length us, event | category | flops | bytes accessed | tf_op | source)
XLA Modules:
  0.0 107.7 jit_solution(545189189110132379)
XLA Ops:
  0.6 102.4 %mixer_backward.1 = (bf16[128,256]{1,0:T(8,128)(2,1)}, bf16[128,512]{1,0:T(8,128)(2,1)}, f32[8,128]{1,0:T(8,128)}, f32[8,128,128]{2,1,0:T(8,128)}) custom-call(bf16[128,256]{1,0:T(8,128)(2,1)} %refs_0_.1, bf16[128,512]{1,0:T(8,128)(2,1)} %refs_1_.1, bf16[128,512]{1,0:T(8,128)(2,1)} %refs_2_.1, bf16[8,128,128]{2,1,0:T(8,128)(2,1)} %refs_3_.1, ...), custom_call_target="tpu_custom_call" | custom-call | tf_op jit(solution)/shard_map/mixer_backward/pallas_call | solution.py:696
  103.1 0.0 copy-start
  103.1 1.5 %copy.16 = bf16[128,256]{1,0:T(8,128)(2,1)} copy(bf16[128,256]{1,0:T(8,128)(2,1)} %get-tuple-element.8) | data formatting | bytes 131072
  104.6 0.0 copy-done
  104.6 0.0 copy-start.1
  104.6 0.7 copy.17
  105.3 0.0 copy-done.1
  105.3 0.6 copy.18
  105.9 1.9 %copy.19 = f32[8,128,128]{2,1,0:T(8,128)} copy(f32[8,128,128]{2,1,0:T(8,128)} %get-tuple-element.11) | data formatting | bytes 1048576
Async XLA Ops:
  103.1 1.5 %copy-start = (bf16[128,512]{1,0:T(8,128)(2,1)S(1)}, bf16[128,512]{1,0:T(8,128)(2,1)}, u32[]{:S(2)}) copy-start(bf16[128,512]{1,0:T(8,128)(2,1)} %get-tuple-element.9) | copy-start | bytes 393220
  104.6 0.7 copy-start.1

commit v3 on v2

--- a/solution.py
+++ b/solution.py
@@ -62,6 +62,7 @@
     wg,
     ig,
     tcol,
+    tpre,
     w_other,
     cot_other,
     b_other,
@@ -116,6 +117,13 @@
     across = lax.rem(k + nk // 2, nk)
     mine = pl.ds(pl.multiple_of(r * CH, CH), CH)
     other = pl.ds(pl.multiple_of((1 - r) * CH, CH), CH)
+    me = r * nk + k
+
+    def piece_of(kk, side):
+        return (
+            pl.ds(pl.multiple_of(kk * rowt, rowt), rowt),
+            pl.ds(pl.multiple_of(side * TOK, TOK), TOK),
+        )
 
     def ztok(zz, rr):
         return lax.rem(zz + nz, nz) * 2 + rr
@@ -227,6 +235,7 @@
                 (cot.at[:, mine], g.at[r]),
                 (c_in.at[k], cs.at[r]),
                 (b_in.at[k], bs.at[r]),
+                (tokens.at[piece_of(k, core)], tpre.at[c]),
             )
         )
     ]
@@ -244,11 +253,12 @@
 
     each(1, nz, lambda j: greet(ztok(z + j, r), c))
     each(1, chips, greet_chip)
+    each(1, nk, lambda j: greet(tok, xor(k, j, nk) * 2 + 1 - core))
     greet(tok, sibling)
     greet(partner, sibling)
     for load in loads:
         load.wait()
-    pl.semaphore_wait(barrier, (nz - 1) + (chips - 1) + 2)
+    pl.semaphore_wait(barrier, (nz - 1) + (chips - 1) + (nk - 1) + 2)
 
     ring_w = Ring(wg, r)
     swap_r = single(raw_own, raw.at[r], partner, c)
@@ -257,12 +267,19 @@
     swap_w = single(w_other, wg.at[z, r], partner, c)
     swap_b = single(b_other, bs.at[r], partner, across * 2 + core)
     swap_r.start()
-    swap_g.start()
-    swap_c.start()
+    swap_w.start()
     ring_w.begin(0)
     ring_w.begin(1)
-    swap_w.start()
+    swap_c.start()
     swap_b.start()
+    swap_g.start()
+
+    def piece_out(j):
+        to = xor(c, j, 2 * nk)
+        return feat.at[(c, r) + piece_of(to // 2, to % 2)], tpre.at[c], tok, to
+
+    pieces = Family(1, 2 * nk, piece_out, tpre.at[pl.ds(0, 2 * nk - 1)])
+    pieces.start()
 
     def feat_out(j):
         rr, kk = chip(j)
@@ -276,8 +293,6 @@
 
     feats = Family(1, chips, feat_out, feat.at[pl.ds(0, chips - 1), 0])
     feats_on = Family(0, chips, feat_on, feat.at[:, 0])
-    feats.start()
-    feats_on.start_one(0)
     raw[r] = raw_own[...]
 
     groups_w = []
@@ -328,9 +343,24 @@
     decays = Family(1, nz, decay_out, dall.at[pl.ds(0, nz - 1)])
     decays.start()
     ring_w.ticks(groups_w[1])
+    swap_w.wait_recv()
+    ring_w.begin(2)
+    ring_w.begin(3)
+
+    def column_out(j):
+        to = lax.rem(z + j, nz)
+        return tpre.at[to], tcol.at[me, core, z], ztok(to, r), c
+
+    pieces.recv()
+    columns_out = Family(1, nz, column_out, tcol.at[0, 0, pl.ds(0, nz - 1)])
+    columns_out.start()
+    tcol[me, core, z] = tpre[z]
+    ring_w.ticks(groups_w[2])
 
     swap_g.wait_recv()
     swap_c.wait_recv()
+    feats.start()
+    feats_on.start_one(0)
     adjoint = []
     for p in range(2):
         gt = g[p].astype(F32).T
@@ -377,10 +407,7 @@
 
     adjoints = Exchange(0, True)
     adjoints.start(adjoint[0] + decay_rows[0] * adjoint[1])
-    swap_w.wait_recv()
-    ring_w.begin(2)
-    ring_w.begin(3)
-    ring_w.ticks(groups_w[2])
+    ring_w.ticks(groups_w[3])
     swap_b.wait_recv()
 
     lower = ids0 >= ids1
@@ -397,17 +424,44 @@
                 gtb[p, i * HEAD : (i + 1) * HEAD, :], kern
             )
 
-    block_kernels(0, (0, 1))
-    ring_w.ticks(groups_w[3][:2])
+    block_kernels(0, (0, 1, 2, 3))
+    ring_w.ticks(groups_w[4])
+    block_kernels(1, (0, 1, 2, 3))
+    ring_w.ticks(groups_w[5])
     decays.recv()
     adjoints.prefix()
-    ring_w.ticks(groups_w[3][2:])
-    block_kernels(0, (2, 3))
-    ring_w.ticks(groups_w[4][:2])
-    block_kernels(1, (0, 1))
-    ring_w.ticks(groups_w[4][2:])
-    block_kernels(1, (2, 3))
-    ring_w.ticks(groups_w[5])
+    ring_w.ticks(groups_w[6])
+    columns_out.recv()
+
+    def tcol_out(j):
+        rr, kk = chip(j)
+        at = tcol.at[me, core]
+        return at, at, z * 2 + rr, kk * 2 + core
+
+    def tcol_on(j):
+        rr, kk = chip(j)
+        at = tcol.at[rr * nk + kk, core]
+        return at, at, tok, sibling
+
+    tcols = Family(1, chips, tcol_out, tcol.at[pl.ds(0, chips - 1), 0])
+    tcols_on = Family(0, chips, tcol_on, tcol.at[:, 0])
+    ring_w.ticks(groups_w[7])
+    feats.recv()
+    each(1, chips, feats_on.start_one)
+    tcols.start()
+    tcols_on.start_one(0)
+    ring_w.ticks(groups_w[8])
+
+    def project(first, last):
+        total = proj[...] if first else jnp.zeros((2 * TOK, CH), F32)
+        for d in range(first, last):
+            for way in (1, -1) if 0 < d < hops else (1,):
+                n = lax.rem(z + way * d + nz, nz)
+                total = total + dot(feat[n].reshape(2 * TOK, CH), wg[n].reshape(CH, CH))
+        proj[...] = total
+
+    feats_on.recv()
+    project(0, hops)
 
     late = adjoints.result()
     ring_i = Ring(ig, 0)
@@ -421,43 +475,8 @@
         ring_i.begin(2 * p)
         ring_i.begin(2 * p + 1)
         igtm[p * TOK : (p + 1) * TOK, :] = grad_low.astype(F32).T.astype(BF16)
-    ring_w.ticks(groups_w[6])
-    feats.recv()
-    each(1, chips, feats_on.start_one)
-    ring_i.ticks(groups_i[0])
-    ring_w.ticks(groups_w[7])
-    feats_on.recv()
-
-    own_rows = pl.ds(pl.multiple_of(k * rowt, rowt), rowt)
-    own_lanes = pl.ds(pl.multiple_of(core * TOK, TOK), TOK)
-    me = r * nk + k
-
-    def column_out(j):
-        to = lax.rem(z + j, nz)
-        src = feat.at[to, r, own_rows, own_lanes]
-        return src, tcol.at[me, core, z], ztok(to, r), c
-
-    own_columns = pltpu.make_async_copy(
-        feat.at[z, r, own_rows, own_lanes], tcol.at[me, core, z], local_sem.at[0]
-    )
-    columns_out = Family(1, nz, column_out, tcol.at[0, 0, pl.ds(0, nz - 1)])
-
-    def project(first, last):
-        total = proj[...] if first else jnp.zeros((2 * TOK, CH), F32)
-        for d in range(first, last):
-            for way in (1, -1) if 0 < d < hops else (1,):
-                n = lax.rem(z + way * d + nz, nz)
-                total = total + dot(feat[n].reshape(2 * TOK, CH), wg[n].reshape(CH, CH))
-        proj[...] = total
-
-    project(0, min(3, hops))
-    if hops > 3:
-        ring_w.ticks(groups_w[8][:1])
-        project(3, 6)
-    ring_w.ticks(groups_w[8][1:] if hops > 3 else groups_w[8])
-    ring_i.ticks(groups_i[1][:2])
     ring_w.ticks(groups_w[9])
-    project(min(6, hops), hops + 1)
+    project(hops, hops + 1)
     states = []
     for p in range(2):
         xt = proj[p * TOK : (p + 1) * TOK, :].astype(BF16).astype(F32).T
@@ -466,9 +485,7 @@
     s_first[...] = states[0]
     scan = Exchange(1, False)
     scan.start(decay_rows[1] * states[0] + states[1])
-    own_columns.start()
-    columns_out.start()
-    ring_i.ticks(groups_i[1][2:])
+    ring_i.ticks(groups_i[0][:2])
 
     def term(kk, side):
         n = kk * 2 + side
@@ -485,32 +502,27 @@
         y_sibs.start_one(j)
 
     each(0, nk // 2, first_terms)
-    ring_i.ticks(groups_i[2][:2])
+    ring_i.ticks(groups_i[0][2:])
     each(nk // 2, nk, first_terms)
-    ring_i.ticks(groups_i[2][2:])
-
-    scan.prefix()
-    own_columns.wait()
-    columns_out.recv()
-
-    def tcol_out(j):
+    ring_i.ticks(groups_i[1][:2])
+    each(0, nk // 2, lambda j: term(j, core))
+    ring_i.ticks(groups_i[1][2:])
+    each(nk // 2, nk, lambda j: term(j, core))
+    y_sibs.recv()
+
+    def y_sum(j):
+        y_out[j] = (y_all[core, j].astype(F32) + y_sib[j].astype(F32)).astype(BF16)
+
+    each(0, nk, y_sum)
+    y_in[0] = y_out[k, r]
+
+    def y_chip(j):
         rr, kk = chip(j)
-        at = tcol.at[me, core]
-        return at, at, z * 2 + rr, kk * 2 + core
-
-    def tcol_on(j):
-        rr, kk = chip(j)
-        at = tcol.at[rr * nk + kk, core]
-        return at, at, tok, sibling
-
-    tcols = Family(1, chips, tcol_out, tcol.at[pl.ds(0, chips - 1), 0])
-    tcols_on = Family(0, chips, tcol_on, tcol.at[:, 0])
-    tcols.start()
-    tcols_on.start_one(0)
-    ring_i.ticks(groups_i[3][:2])
-    each(0, nk // 2, lambda j: term(j, core))
-    ring_i.ticks(groups_i[3][2:])
-    each(nk // 2, nk, lambda j: term(j, core))
+        return y_out.at[kk, rr], y_in.at[j], z * 2 + rr, kk * 2 + core
+
+    y_outs = Family(1, chips, y_chip, y_in.at[pl.ds(1, chips - 1)])
+    y_outs.start()
+    ring_i.ticks(groups_i[2])
 
     rowsums = jnp.zeros((TOK, TOK), F32)
     colsums, ends, maps = [], [], []
@@ -533,11 +545,32 @@
 
     for p in range(2):
         pair_sum = jnp.zeros((TOK, TOK), F32)
-        pair_sum, rowsums = pairs(p, (0, 1), pair_sum, rowsums)
-        ring_i.ticks(groups_i[4][2 * p : 2 * p + 2])
-        pair_sum, rowsums = pairs(p, (2, 3), pair_sum, rowsums)
+        pair_sum, rowsums = pairs(p, (0, 1, 2, 3), pair_sum, rowsums)
         maps.append(dot2(pair_sum, bs[p]))
+        ring_i.ticks(groups_i[3][2 * p : 2 * p + 2])
     rowsums = rowsums.T[0 : 2 * HALF]
+    scan.prefix()
+    tcols.recv()
+    each(1, chips, tcols_on.start_one)
+    ring_i.ticks(groups_i[4])
+
+    def gather(first, last):
+        for half in range(2):
+            total = wtot[half] if first else jnp.zeros((CH, TOK), F32)
+            for d in range(first, last):
+                for way in (1, -1) if 0 < d < hops else (1,):
+                    n = lax.rem(z + way * d + nz, nz)
+                    for p in range(2):
+                        cols = tcol[p * nk : (p + 1) * nk, half, n].reshape(TOK, TOK)
+                        total = total + dot(ig[n, p], cols)
+            wtot[half] = total
+
+    tcols_on.recv()
+    gather(0, min(4, hops))
+    ring_i.ticks(groups_i[5])
+    gather(min(4, hops), min(6, hops))
+    ring_i.ticks(groups_i[6])
+    gather(min(6, hops), hops)
 
     early = scan.result()
     state_at = [early, decay_rows[0] * early + s_first[...]]
@@ -562,21 +595,13 @@
 
     map_parts = Family(1, 4, map_to, m_in.at[pl.ds(1, 3)])
     map_parts.start()
-    ring_i.ticks(groups_i[5])
-
-    def y_sum(j):
-        y_out[j] = (y_all[core, j].astype(F32) + y_sib[j].astype(F32)).astype(BF16)
-
-    y_sibs.recv()
-    each(0, nk, y_sum)
-    y_in[0] = y_out[k, r]
-
-    def y_chip(j):
-        rr, kk = chip(j)
-        return y_out.at[kk, rr], y_in.at[j], z * 2 + rr, kk * 2 + core
-
-    y_outs = Family(1, chips, y_chip, y_in.at[pl.ds(1, chips - 1)])
-    y_outs.start()
+    ring_i.ticks(groups_i[7])
+    gather(hops, hops + 1)
+    for half in range(2):
+        wgrad[half] = wtot[half].T.astype(BF16)
+    swap_o = single(wgrad.at[1 - r], weight_grad.at[:, mine], partner, c)
+    swap_o.start()
+    weight_grad[:, mine] = wgrad[r]
 
     for n, parts in enumerate((colsums, ends, starts, corners)):
         for q in range(2 * HALF):
@@ -600,60 +625,27 @@
     swap_s.start()
 
     map_parts.recv()
-    m_groups[k, core] = (m_own[r, core] + m_in[1] + m_in[2] + m_in[3]).astype(BF16)
+    m_groups[c] = (m_own[r, core] + m_in[1] + m_in[2] + m_in[3]).astype(BF16)
 
     def map_out(j):
-        at = m_groups.at[k, core]
-        return at, at, tok, xor(k, j, nk) * 2 + core
-
-    def map_on(j):
-        at = m_groups.at[xor(k, j, nk), core]
-        return at, at, tok, sibling
-
-    map_outs = Family(1, nk, map_out, m_groups.at[pl.ds(0, nk - 1), 0])
-    map_ons = Family(0, nk, map_on, m_groups.at[:, 0])
+        return m_groups.at[c], m_groups.at[c], tok, xor(c, j, 2 * nk)
+
+    map_outs = Family(1, 2 * nk, map_out, m_groups.at[pl.ds(0, 2 * nk - 1)])
     map_outs.start()
-    map_ons.start_one(0)
-    ring_i.ticks(groups_i[6][:2])
-    tcols.recv()
-    each(1, chips, tcols_on.start_one)
-    ring_i.ticks(groups_i[6][2:])
-
-    def gather(first, last):
-        for half in range(2):
-            total = wtot[half] if first else jnp.zeros((CH, TOK), F32)
-            for d in range(first, last):
-                for way in (1, -1) if 0 < d < hops else (1,):
-                    n = lax.rem(z + way * d + nz, nz)
-                    for p in range(2):
-                        cols = tcol[p * nk : (p + 1) * nk, half, n].reshape(TOK, TOK)
-                        total = total + dot(ig[n, p], cols)
-            wtot[half] = total
-
+
+    y_outs.recv()
+    total = y_in[0].astype(F32)
+    for j in range(1, chips):
+        total = total + y_in[j].astype(F32)
+    token_grad[...] = total.astype(BF16)
     swap_s.wait_recv()
     own = jnp.where(low_half, s_out[0], s_out[1])
     sub = lax.broadcasted_iota(jnp.int32, (2 * HALF, TOK), 0)
     step_grad[...] = jnp.where((sub < HALF) == low_half, own, s_swap[...])
     map_outs.recv()
-    each(1, nk, map_ons.start_one)
-    tcols_on.recv()
-    gather(0, hops)
-    ring_i.ticks(groups_i[7])
-    gather(hops, hops + 1)
-    for half in range(2):
-        wgrad[half] = wtot[half].T.astype(BF16)
-    swap_o = single(wgrad.at[1 - r], weight_grad.at[:, mine], partner, c)
-    swap_o.start()
-    weight_grad[:, mine] = wgrad[r]
-
-    y_outs.recv()
-    total = y_in[0].astype(F32)
-    for j in range(1, chips):
-        total = total + y_in[j].astype(F32)
-    token_grad[...] = total.astype(BF16)
-    map_ons.recv()
-    for gg in range(nk):
-        map_grad[gg] = m_groups[gg].reshape(TOK, STATE).astype(F32)
+    for n in range(2 * nk):
+        rows = slice((n % 2) * (TOK // 2), (n % 2 + 1) * (TOK // 2))
+        map_grad[n // 2, rows, :] = m_groups[n].astype(F32)
 
     for swap in (swap_r, swap_g, swap_c, swap_b, swap_w, swap_s):
         swap.wait_send()
@@ -674,7 +666,7 @@
         y_outs,
         map_parts,
         map_outs,
-        map_ons,
+        pieces,
     ):
         family.sent()
     swap_o.wait_recv()
@@ -708,6 +700,7 @@
             v((nz, 2, TOK, CH), BF16),
             v((nz, 2, CH, TOK), BF16),
             v((2 * nk, 2, nz, rowt, TOK), BF16),
+            v((2 * nk, rowt, TOK), BF16),
             v((TOK, CH), BF16),
             v((TOK, CH), BF16),
             v((TOK, STATE), BF16),
@@ -742,11 +735,11 @@
             v((chips, TOK, CH), BF16),
             v((2, 2, TOK // 2, STATE), F32),
             v((4, TOK // 2, STATE), F32),
-            v((nk, 2, TOK // 2, STATE), BF16),
+            v((2 * nk, TOK // 2, STATE), BF16),
             v((2, 2 * HALF, TOK), F32),
             v((2 * HALF, TOK), F32),
             v((2, TOK, CH), BF16),
-            pltpu.SemaphoreType.DMA((10,)),
+            pltpu.SemaphoreType.DMA((11,)),
             pltpu.SemaphoreType.DMA((24,)),
             pltpu.SemaphoreType.DMA((22 + 16 * (nz // 2 + 1),)),
         ],

time: 110 us -> 107 us (0.973); the launches traced: 108 us -> 107 us
  no operation moved by 1% of the time
where the time goes in v3:
time: 107 us
  Pallas kernels  102 us (95%)
  local copies, waits for them, and re-layouts  4.65 us (4%)
    pallas_call x1, Pallas kernels, local(): pl.pallas_call(body, out_shape=(jax.ShapeDtypeStruct((TOK, CH), BF16), ja...  102 us
    unnamed x8, local copies, waits for them, and re-layouts  4.65 us

profile of v3, /device:TPU:1, one launch (start us, length us, event | category | flops | bytes accessed | tf_op | source)
XLA Modules:
  0.0 106.9 jit_solution(10692676377537748583)
XLA Ops:
  0.6 101.6 %mixer_backward.1 = (bf16[128,256]{1,0:T(8,128)(2,1)}, bf16[128,512]{1,0:T(8,128)(2,1)}, f32[8,128]{1,0:T(8,128)}, f32[8,128,128]{2,1,0:T(8,128)}) custom-call(bf16[128,256]{1,0:T(8,128)(2,1)} %refs_0_.1, bf16[128,512]{1,0:T(8,128)(2,1)} %refs_1_.1, bf16[128,512]{1,0:T(8,128)(2,1)} %refs_2_.1, bf16[8,128,128]{2,1,0:T(8,128)(2,1)} %refs_3_.1, ...), custom_call_target="tpu_custom_call" | custom-call | tf_op jit(solution)/shard_map/mixer_backward/pallas_call | solution.py:688
  102.2 0.0 copy-start
  102.2 1.5 %copy.16 = bf16[128,256]{1,0:T(8,128)(2,1)} copy(bf16[128,256]{1,0:T(8,128)(2,1)} %get-tuple-element.8) | data formatting | bytes 131072
  103.7 0.0 copy-done
  103.7 0.0 copy-start.1
  103.8 0.7 copy.17
  104.4 0.0 copy-done.1
  104.4 0.6 copy.18
  105.0 1.9 %copy.19 = f32[8,128,128]{2,1,0:T(8,128)} copy(f32[8,128,128]{2,1,0:T(8,128)} %get-tuple-element.11) | data formatting | bytes 1048576
Async XLA Ops:
  102.2 1.5 %copy-start = (bf16[128,512]{1,0:T(8,128)(2,1)S(1)}, bf16[128,512]{1,0:T(8,128)(2,1)}, u32[]{:S(2)}) copy-start(bf16[128,512]{1,0:T(8,128)(2,1)} %get-tuple-element.9) | copy-start | bytes 393220
  103.7 0.7 copy-start.1

commit v4 on v3

--- a/solution.py
+++ b/solution.py
@@ -65,6 +65,7 @@
     tpre,
     w_other,
     cot_other,
+    g_relay,
     b_other,
     c_other,
     raw_own,
@@ -115,6 +116,9 @@
     partner = z * 2 + 1 - r
     sibling = c + 1 - 2 * core
     across = lax.rem(k + nk // 2, nk)
+    low = k // (nk // 2)
+    r_before = low * r + (1 - low) * (1 - r)
+    r_after = low * (1 - r) + (1 - low) * r
     mine = pl.ds(pl.multiple_of(r * CH, CH), CH)
     other = pl.ds(pl.multiple_of((1 - r) * CH, CH), CH)
     me = r * nk + k
@@ -262,17 +266,18 @@
 
     ring_w = Ring(wg, r)
     swap_r = single(raw_own, raw.at[r], partner, c)
-    swap_g = single(cot_other, g.at[r], partner, c)
+    swap_g = single(cot_other, g_relay, z * 2 + r_before, across * 2 + core)
+    relay_g = single(g_relay, g.at[r_after], z * 2 + r_before, across * 2 + core)
     swap_c = single(c_other, cs.at[r], partner, across * 2 + core)
     swap_w = single(w_other, wg.at[z, r], partner, c)
     swap_b = single(b_other, bs.at[r], partner, across * 2 + core)
     swap_r.start()
+    swap_g.start()
     swap_w.start()
     ring_w.begin(0)
     ring_w.begin(1)
     swap_c.start()
     swap_b.start()
-    swap_g.start()
 
     def piece_out(j):
         to = xor(c, j, 2 * nk)
@@ -295,15 +300,19 @@
     feats_on = Family(0, chips, feat_on, feat.at[:, 0])
     raw[r] = raw_own[...]
 
-    groups_w = []
-    for t in range(1, hops + 3):
-        group = [(t, 0), (t, 1)] if t <= hops else []
-        groups_w.append(group + ([(t - 2, 2), (t - 2, 3)] if t > 2 else []))
-    groups_w += [[]] * (10 - len(groups_w))
-    groups_i = [[(s, n) for n in range(4)] for s in range(1, hops)]
-    groups_i += [[]] * (7 - len(groups_i)) + [[(hops, n) for n in range(4)]]
-
-    ring_w.ticks(groups_w[0])
+    def own(t):
+        if t <= hops:
+            ring_w.ticks([(t, 0), (t, 1)])
+
+    def far(t):
+        if t <= hops:
+            ring_w.ticks([(t, 2), (t, 3)])
+
+    def grads(t):
+        if t < hops or t == 8:
+            ring_i.ticks([(min(t, hops), n) for n in range(4)])
+
+    own(1)
     swap_r.wait_recv()
 
     low_half = r == 0
@@ -332,35 +341,25 @@
     block_decay = jnp.exp(log_total)
     decay_rows = [heads_to_rows(block_decay, p) for p in range(2)]
     columns = jnp.concatenate([log_decay, jnp.zeros((TOK - 2 * HALF, TOK), F32)], axis=0).T
-    dtile[...] = jnp.concatenate(
-        [block_decay[0:HALF] * block_decay[HALF : 2 * HALF], jnp.zeros((HALF, TOK), F32)], axis=0
-    )
-    dall[z] = dtile[...]
+    lane = lax.broadcasted_iota(jnp.int32, (1, TOK), 1)
+    decay_row = jnp.zeros((1, TOK), F32)
+    for i in range(HALF):
+        decay_row = jnp.where(
+            lane == i, block_decay[i : i + 1] * block_decay[HALF + i : HALF + i + 1], decay_row
+        )
+    dtile[...] = decay_row
+    dall[z] = decay_row
 
     def decay_out(j):
         return dtile, dall.at[z], ztok(z + j, r), c
 
     decays = Family(1, nz, decay_out, dall.at[pl.ds(0, nz - 1)])
     decays.start()
-    ring_w.ticks(groups_w[1])
-    swap_w.wait_recv()
-    ring_w.begin(2)
-    ring_w.begin(3)
-
-    def column_out(j):
-        to = lax.rem(z + j, nz)
-        return tpre.at[to], tcol.at[me, core, z], ztok(to, r), c
-
-    pieces.recv()
-    columns_out = Family(1, nz, column_out, tcol.at[0, 0, pl.ds(0, nz - 1)])
-    columns_out.start()
-    tcol[me, core, z] = tpre[z]
-    ring_w.ticks(groups_w[2])
-
     swap_g.wait_recv()
+    relay_g.start()
+    own(2)
+    relay_g.wait_recv()
     swap_c.wait_recv()
-    feats.start()
-    feats_on.start_one(0)
     adjoint = []
     for p in range(2):
         gt = g[p].astype(F32).T
@@ -395,9 +394,11 @@
             head = (z * piece) // HEAD
             self.out.recv()
             carry = jnp.zeros((piece, STATE), F32)
+            own = jnp.where(lane == head, dall[...].reshape(nz, TOK), 0.0)
+            decay = jnp.broadcast_to(jnp.sum(own, axis=1, keepdims=True), (nz, STATE))
             for at in reversed(range(nz)) if self.reverse else range(nz):
                 back_state[n, at] = carry.astype(BF16)
-                carry = dall[at, pl.ds(head, 1), :] * carry + recv_state[n, at].astype(F32)
+                carry = decay[at : at + 1] * carry + recv_state[n, at].astype(F32)
             self.back.start()
             state_in[n, z] = back_state[n, z]
 
@@ -407,7 +408,12 @@
 
     adjoints = Exchange(0, True)
     adjoints.start(adjoint[0] + decay_rows[0] * adjoint[1])
-    ring_w.ticks(groups_w[3])
+    swap_w.wait_recv()
+    ring_w.begin(2)
+    ring_w.begin(3)
+    own(3)
+    feats.start()
+    feats_on.start_one(0)
     swap_b.wait_recv()
 
     lower = ids0 >= ids1
@@ -425,13 +431,26 @@
             )
 
     block_kernels(0, (0, 1, 2, 3))
-    ring_w.ticks(groups_w[4])
+    far(1)
+    own(4)
     block_kernels(1, (0, 1, 2, 3))
-    ring_w.ticks(groups_w[5])
     decays.recv()
     adjoints.prefix()
-    ring_w.ticks(groups_w[6])
-    columns_out.recv()
+    far(2)
+    own(5)
+
+    def column_out(j):
+        to = lax.rem(z + j, nz)
+        return tpre.at[to], tcol.at[me, core, z], ztok(to, r), c
+
+    pieces.recv()
+    columns_out = Family(1, nz, column_out, tcol.at[0, 0, pl.ds(0, nz - 1)])
+    columns_out.start()
+    tcol[me, core, z] = tpre[z]
+    far(3)
+    own(6)
+    far(4)
+    own(7)
 
     def tcol_out(j):
         rr, kk = chip(j)
@@ -445,13 +464,6 @@
 
     tcols = Family(1, chips, tcol_out, tcol.at[pl.ds(0, chips - 1), 0])
     tcols_on = Family(0, chips, tcol_on, tcol.at[:, 0])
-    ring_w.ticks(groups_w[7])
-    feats.recv()
-    each(1, chips, feats_on.start_one)
-    tcols.start()
-    tcols_on.start_one(0)
-    ring_w.ticks(groups_w[8])
-
     def project(first, last):
         total = proj[...] if first else jnp.zeros((2 * TOK, CH), F32)
         for d in range(first, last):
@@ -459,9 +471,6 @@
                 n = lax.rem(z + way * d + nz, nz)
                 total = total + dot(feat[n].reshape(2 * TOK, CH), wg[n].reshape(CH, CH))
         proj[...] = total
-
-    feats_on.recv()
-    project(0, hops)
 
     late = adjoints.result()
     ring_i = Ring(ig, 0)
@@ -475,8 +484,22 @@
         ring_i.begin(2 * p)
         ring_i.begin(2 * p + 1)
         igtm[p * TOK : (p + 1) * TOK, :] = grad_low.astype(F32).T.astype(BF16)
-    ring_w.ticks(groups_w[9])
-    project(hops, hops + 1)
+    far(5)
+    own(8)
+    feats.recv()
+    each(1, chips, feats_on.start_one)
+    columns_out.recv()
+    tcols.start()
+    tcols_on.start_one(0)
+    far(6)
+    grads(1)
+    feats_on.recv()
+    project(0, min(6, hops))
+    far(7)
+    grads(2)
+    project(min(6, hops), min(7, hops))
+    far(8)
+    project(min(7, hops), hops + 1)
     states = []
     for p in range(2):
         xt = proj[p * TOK : (p + 1) * TOK, :].astype(BF16).astype(F32).T
@@ -485,7 +508,7 @@
     s_first[...] = states[0]
     scan = Exchange(1, False)
     scan.start(decay_rows[1] * states[0] + states[1])
-    ring_i.ticks(groups_i[0][:2])
+    grads(3)
 
     def term(kk, side):
         n = kk * 2 + side
@@ -502,12 +525,9 @@
         y_sibs.start_one(j)
 
     each(0, nk // 2, first_terms)
-    ring_i.ticks(groups_i[0][2:])
     each(nk // 2, nk, first_terms)
-    ring_i.ticks(groups_i[1][:2])
-    each(0, nk // 2, lambda j: term(j, core))
-    ring_i.ticks(groups_i[1][2:])
-    each(nk // 2, nk, lambda j: term(j, core))
+    grads(4)
+    each(0, nk, lambda j: term(j, core))
     y_sibs.recv()
 
     def y_sum(j):
@@ -522,7 +542,7 @@
 
     y_outs = Family(1, chips, y_chip, y_in.at[pl.ds(1, chips - 1)])
     y_outs.start()
-    ring_i.ticks(groups_i[2])
+    grads(5)
 
     rowsums = jnp.zeros((TOK, TOK), F32)
     colsums, ends, maps = [], [], []
@@ -547,30 +567,26 @@
         pair_sum = jnp.zeros((TOK, TOK), F32)
         pair_sum, rowsums = pairs(p, (0, 1, 2, 3), pair_sum, rowsums)
         maps.append(dot2(pair_sum, bs[p]))
-        ring_i.ticks(groups_i[3][2 * p : 2 * p + 2])
+        if p == 0:
+            scan.prefix()
     rowsums = rowsums.T[0 : 2 * HALF]
-    scan.prefix()
+    grads(6)
     tcols.recv()
     each(1, chips, tcols_on.start_one)
-    ring_i.ticks(groups_i[4])
 
     def gather(first, last):
-        for half in range(2):
-            total = wtot[half] if first else jnp.zeros((CH, TOK), F32)
-            for d in range(first, last):
-                for way in (1, -1) if 0 < d < hops else (1,):
-                    n = lax.rem(z + way * d + nz, nz)
-                    for p in range(2):
-                        cols = tcol[p * nk : (p + 1) * nk, half, n].reshape(TOK, TOK)
-                        total = total + dot(ig[n, p], cols)
-            wtot[half] = total
-
+        total = wtot[...] if first else jnp.zeros((CH, 2 * TOK), F32)
+        for d in range(first, last):
+            for way in (1, -1) if 0 < d < hops else (1,):
+                n = lax.rem(z + way * d + nz, nz)
+                grad = jnp.concatenate([ig[n, 0], ig[n, 1]], axis=1)
+                cols = [tcol[:, half, n].reshape(2 * TOK, TOK) for half in range(2)]
+                total = total + dot(grad, jnp.concatenate(cols, axis=1))
+        wtot[...] = total
+
+    grads(7)
     tcols_on.recv()
-    gather(0, min(4, hops))
-    ring_i.ticks(groups_i[5])
-    gather(min(4, hops), min(6, hops))
-    ring_i.ticks(groups_i[6])
-    gather(min(6, hops), hops)
+    gather(0, hops)
 
     early = scan.result()
     state_at = [early, decay_rows[0] * early + s_first[...]]
@@ -595,10 +611,10 @@
 
     map_parts = Family(1, 4, map_to, m_in.at[pl.ds(1, 3)])
     map_parts.start()
-    ring_i.ticks(groups_i[7])
+    grads(8)
     gather(hops, hops + 1)
     for half in range(2):
-        wgrad[half] = wtot[half].T.astype(BF16)
+        wgrad[half] = wtot[:, half * TOK : (half + 1) * TOK].T.astype(BF16)
     swap_o = single(wgrad.at[1 - r], weight_grad.at[:, mine], partner, c)
     swap_o.start()
     weight_grad[:, mine] = wgrad[r]
@@ -639,15 +655,15 @@
         total = total + y_in[j].astype(F32)
     token_grad[...] = total.astype(BF16)
     swap_s.wait_recv()
-    own = jnp.where(low_half, s_out[0], s_out[1])
+    kept = jnp.where(low_half, s_out[0], s_out[1])
     sub = lax.broadcasted_iota(jnp.int32, (2 * HALF, TOK), 0)
-    step_grad[...] = jnp.where((sub < HALF) == low_half, own, s_swap[...])
+    step_grad[...] = jnp.where((sub < HALF) == low_half, kept, s_swap[...])
     map_outs.recv()
     for n in range(2 * nk):
         rows = slice((n % 2) * (TOK // 2), (n % 2 + 1) * (TOK // 2))
         map_grad[n // 2, rows, :] = m_groups[n].astype(F32)
 
-    for swap in (swap_r, swap_g, swap_c, swap_b, swap_w, swap_s):
+    for swap in (swap_r, swap_g, relay_g, swap_c, swap_b, swap_w, swap_s):
         swap.wait_send()
     ring_w.sent()
     ring_i.sent()
@@ -685,7 +701,7 @@
     def body(*refs):
         kernel(nz, nk, *refs)
 
-    return pl.pallas_call(
+    results = pl.pallas_call(
         body,
         out_shape=(
             jax.ShapeDtypeStruct((TOK, CH), BF16),
@@ -703,6 +719,7 @@
             v((2 * nk, rowt, TOK), BF16),
             v((TOK, CH), BF16),
             v((TOK, CH), BF16),
+            v((TOK, CH), BF16),
             v((TOK, STATE), BF16),
             v((TOK, STATE), BF16),
             v((2 * HALF, TOK), F32),
@@ -710,8 +727,8 @@
             v((2, TOK, STATE), BF16),
             v((2, TOK, STATE), BF16),
             v((2, 2 * HALF, TOK), F32),
-            v((2 * HALF, TOK), F32),
-            v((nz, 2 * HALF, TOK), F32),
+            v((1, TOK), F32),
+            v((nz, 1, TOK), F32),
             v((2, nz, piece, STATE), BF16),
             v((2, nz, piece, STATE), BF16),
             v((2, nz, piece, STATE), BF16),
@@ -728,7 +745,7 @@
             v((6, 2 * HALF, TOK), F32),
             v((2 * TOK, CH), BF16),
             v((2 * TOK, CH), F32),
-            v((2, CH, TOK), F32),
+            v((CH, 2 * TOK), F32),
             v((2, nk, 2, TOK, CH), BF16),
             v((nk, 2, TOK, CH), BF16),
             v((nk, 2, TOK, CH), BF16),
@@ -740,14 +757,33 @@
             v((2 * HALF, TOK), F32),
             v((2, TOK, CH), BF16),
             pltpu.SemaphoreType.DMA((11,)),
-            pltpu.SemaphoreType.DMA((24,)),
-            pltpu.SemaphoreType.DMA((22 + 16 * (nz // 2 + 1),)),
+            pltpu.SemaphoreType.DMA((25,)),
+            pltpu.SemaphoreType.DMA((23 + 16 * (nz // 2 + 1),)),
         ],
         compiler_params=pltpu.CompilerParams(
             collective_id=0, has_side_effects=True, vmem_limit_bytes=60 * 1024 * 1024
         ),
         name="mixer_backward",
     )(tokens, w, cot, b, c, raw, rate_log.reshape(1, 2 * HALF), skip.reshape(1, 2 * HALF))
+
+    def hand_over(*refs):
+        copies = [
+            pltpu.make_async_copy(refs[n], refs[4 + n], refs[8].at[n]) for n in range(4)
+        ]
+        for copy in copies:
+            copy.start()
+        for copy in copies:
+            copy.wait()
+
+    return pl.pallas_call(
+        hand_over,
+        out_shape=tuple(jax.ShapeDtypeStruct(a.shape, a.dtype) for a in results),
+        in_specs=[hbm] * 4,
+        out_specs=(hbm,) * 4,
+        scratch_shapes=[pltpu.SemaphoreType.DMA((4,))],
+        compiler_params=pltpu.CompilerParams(vmem_limit_bytes=60 * 1024 * 1024),
+        name="outputs",
+    )(*results)
 
 
 def solution(mesh):

time: 107 us -> 122 us (1.14)
  Pallas kernels: 102 us -> 121 us
  local copies, waits for them, and re-layouts: 4.65 us -> 0 us
    pallas_call x0 -> x1, Pallas kernels: none -> 23.1 us  [local(): pl.pallas_call(hand_over, out_shape=tuple((jax.ShapeDtypeStruct(a.shape,...]
    unnamed x8 -> x0, local copies, waits for them, and re-layouts: 4.65 us -> none
    pallas_call x1, Pallas kernels: 102 us -> 98.1 us  [local(): pl.pallas_call(body, out_shape=(jax.ShapeDtypeStruct((TOK, CH), BF16), ja...]
where the time goes in v4:
time: 122 us
  Pallas kernels  121 us (99%)
    pallas_call x1, Pallas kernels, local(): pl.pallas_call(body, out_shape=(jax.ShapeDtypeStruct((TOK, CH), BF16), ja...  98.1 us
    pallas_call x1, Pallas kernels, local(): pl.pallas_call(hand_over, out_shape=tuple((jax.ShapeDtypeStruct(a.shape,...  23.1 us

profile of v4, /device:TPU:1, one launch (start us, length us, event | category | flops | bytes accessed | tf_op | source)
XLA Modules:
  0.0 121.8 jit_solution(11017462951979130748)
XLA Ops:
  0.6 98.1 %mixer_backward.1 = (bf16[128,256]{1,0:T(8,128)(2,1)}, bf16[128,512]{1,0:T(8,128)(2,1)}, f32[8,128]{1,0:T(8,128)}, f32[8,128,128]{2,1,0:T(8,128)}) custom-call(bf16[128,256]{1,0:T(8,128)(2,1)} %refs_0_.1, bf16[128,512]{1,0:T(8,128)(2,1)} %refs_1_.1, bf16[128,512]{1,0:T(8,128)(2,1)} %refs_2_.1, bf16[8,128,128]{2,1,0:T(8,128)(2,1)} %refs_3_.1, ...), custom_call_target="tpu_custom_call" | custom-call | tf_op jit(solution)/shard_map/mixer_backward/pallas_call | solution.py:704
  98.7 23.1 %outputs.1 = (bf16[128,256]{1,0:T(8,128)(2,1)}, bf16[128,512]{1,0:T(8,128)(2,1)}, f32[8,128]{1,0:T(8,128)}, f32[8,128,128]{2,1,0:T(8,128)}) custom-call(bf16[128,256]{1,0:T(8,128)(2,1)} %get-tuple-element.8.refs_0_, bf16[128,512]{1,0:T(8,128)(2,1)} %get-tuple-element.9.refs_1_, f32[8,128]{1,0:T(8,128)} %get-tuple-element.10.refs_2_, ...), custom_call_target="tpu_custom_call" | custom-call | tf_op jit(solution)/shard_map/outputs/pallas_call | solution.py:778

commit v5 on v4

--- a/solution.py
+++ b/solution.py
@@ -430,27 +430,11 @@
                 gtb[p, i * HEAD : (i + 1) * HEAD, :], kern
             )
 
-    block_kernels(0, (0, 1, 2, 3))
-    far(1)
-    own(4)
-    block_kernels(1, (0, 1, 2, 3))
-    decays.recv()
-    adjoints.prefix()
-    far(2)
-    own(5)
+    kept = {}
 
     def column_out(j):
         to = lax.rem(z + j, nz)
         return tpre.at[to], tcol.at[me, core, z], ztok(to, r), c
-
-    pieces.recv()
-    columns_out = Family(1, nz, column_out, tcol.at[0, 0, pl.ds(0, nz - 1)])
-    columns_out.start()
-    tcol[me, core, z] = tpre[z]
-    far(3)
-    own(6)
-    far(4)
-    own(7)
 
     def tcol_out(j):
         rr, kk = chip(j)
@@ -462,9 +446,45 @@
         at = tcol.at[rr * nk + kk, core]
         return at, at, tok, sibling
 
+    columns_out = Family(1, nz, column_out, tcol.at[0, 0, pl.ds(0, nz - 1)])
     tcols = Family(1, chips, tcol_out, tcol.at[pl.ds(0, chips - 1), 0])
     tcols_on = Family(0, chips, tcol_on, tcol.at[:, 0])
+    ring_i = Ring(ig, 0)
+    scan = Exchange(1, False)
+
+    def adjoint_prefix():
+        decays.recv()
+        adjoints.prefix()
+
+    def columns_start():
+        pieces.recv()
+        columns_out.start()
+        tcol[me, core, z] = tpre[z]
+
+    def columns_spread():
+        columns_out.recv()
+        tcols.start()
+        tcols_on.start_one(0)
+
+    def features_on():
+        feats.recv()
+        each(1, chips, feats_on.start_one)
+
+    def input_grads():
+        late = adjoints.result()
+        kept["adjoint"] = adjoint_at = [decay_rows[1] * late + a_last[...], late]
+        for p in range(2):
+            abt[p] = dot2(adjoint_at[p], bs[p], NT)
+            back = back_local[p] + heads_to_rows(end_decay, p) * abt[p]
+            grad = heads_to_rows(skips, p) * gtb[p].astype(F32) + heads_to_rows(steps, p) * back
+            grad_low = grad.astype(BF16)
+            ig[z, p] = grad_low
+            ring_i.begin(2 * p)
+            ring_i.begin(2 * p + 1)
+            igtm[p * TOK : (p + 1) * TOK, :] = grad_low.astype(F32).T.astype(BF16)
+
     def project(first, last):
+        last = min(last, hops + 1)
         total = proj[...] if first else jnp.zeros((2 * TOK, CH), F32)
         for d in range(first, last):
             for way in (1, -1) if 0 < d < hops else (1,):
@@ -472,43 +492,14 @@
                 total = total + dot(feat[n].reshape(2 * TOK, CH), wg[n].reshape(CH, CH))
         proj[...] = total
 
-    late = adjoints.result()
-    ring_i = Ring(ig, 0)
-    adjoint_at = [decay_rows[1] * late + a_last[...], late]
-    for p in range(2):
-        abt[p] = dot2(adjoint_at[p], bs[p], NT)
-        back = back_local[p] + heads_to_rows(end_decay, p) * abt[p]
-        grad = heads_to_rows(skips, p) * gtb[p].astype(F32) + heads_to_rows(steps, p) * back
-        grad_low = grad.astype(BF16)
-        ig[z, p] = grad_low
-        ring_i.begin(2 * p)
-        ring_i.begin(2 * p + 1)
-        igtm[p * TOK : (p + 1) * TOK, :] = grad_low.astype(F32).T.astype(BF16)
-    far(5)
-    own(8)
-    feats.recv()
-    each(1, chips, feats_on.start_one)
-    columns_out.recv()
-    tcols.start()
-    tcols_on.start_one(0)
-    far(6)
-    grads(1)
-    feats_on.recv()
-    project(0, min(6, hops))
-    far(7)
-    grads(2)
-    project(min(6, hops), min(7, hops))
-    far(8)
-    project(min(7, hops), hops + 1)
-    states = []
-    for p in range(2):
-        xt = proj[p * TOK : (p + 1) * TOK, :].astype(BF16).astype(F32).T
-        xtb[p] = xt.astype(BF16)
-        states.append(dot2(xt * heads_to_rows(end_weight, p), bs[p]))
-    s_first[...] = states[0]
-    scan = Exchange(1, False)
-    scan.start(decay_rows[1] * states[0] + states[1])
-    grads(3)
+    def scan_start():
+        states = []
+        for p in range(2):
+            xt = proj[p * TOK : (p + 1) * TOK, :].astype(BF16).astype(F32).T
+            xtb[p] = xt.astype(BF16)
+            states.append(dot2(xt * heads_to_rows(end_weight, p), bs[p]))
+        s_first[...] = states[0]
+        scan.start(decay_rows[1] * states[0] + states[1])
 
     def term(kk, side):
         n = kk * 2 + side
@@ -518,31 +509,78 @@
     def y_to_sibling(j):
         return y_all.at[1 - core, j], y_sib.at[j], tok, sibling
 
-    y_sibs = Family(0, nk, y_to_sibling, y_sib)
-
-    def first_terms(j):
-        term(j, 1 - core)
-        y_sibs.start_one(j)
-
-    each(0, nk // 2, first_terms)
-    each(nk // 2, nk, first_terms)
-    grads(4)
-    each(0, nk, lambda j: term(j, core))
-    y_sibs.recv()
-
-    def y_sum(j):
-        y_out[j] = (y_all[core, j].astype(F32) + y_sib[j].astype(F32)).astype(BF16)
-
-    each(0, nk, y_sum)
-    y_in[0] = y_out[k, r]
-
     def y_chip(j):
         rr, kk = chip(j)
         return y_out.at[kk, rr], y_in.at[j], z * 2 + rr, kk * 2 + core
 
+    y_sibs = Family(0, nk, y_to_sibling, y_sib)
     y_outs = Family(1, chips, y_chip, y_in.at[pl.ds(1, chips - 1)])
-    y_outs.start()
+
+    def first_terms():
+        def one(j):
+            term(j, 1 - core)
+            y_sibs.start_one(j)
+
+        each(0, nk, one)
+
+    def own_terms():
+        each(0, nk, lambda j: term(j, core))
+
+    def y_sums():
+        def one(j):
+            y_out[j] = (y_all[core, j].astype(F32) + y_sib[j].astype(F32)).astype(BF16)
+
+        y_sibs.recv()
+        each(0, nk, one)
+        y_in[0] = y_out[k, r]
+        y_outs.start()
+
+    def gather(first, last):
+        last = min(last, hops + 1)
+        total = wtot[...] if first else jnp.zeros((CH, 2 * TOK), F32)
+        for d in range(first, last):
+            for way in (1, -1) if 0 < d < hops else (1,):
+                n = lax.rem(z + way * d + nz, nz)
+                grad = jnp.concatenate([ig[n, 0], ig[n, 1]], axis=1)
+                cols = [tcol[:, half, n].reshape(2 * TOK, TOK) for half in range(2)]
+                total = total + dot(grad, jnp.concatenate(cols, axis=1))
+        wtot[...] = total
+
+    block_kernels(0, (0, 1, 2, 3))
+    far(1)
+    own(4)
+    block_kernels(1, (0, 1, 2, 3))
+    adjoint_prefix()
+    far(2)
+    own(5)
+    columns_start()
+    far(3)
+    own(6)
+    far(4)
+    own(7)
+    input_grads()
+    far(5)
+    own(8)
+    features_on()
+    columns_spread()
+    far(6)
+    grads(1)
+    feats_on.recv()
+    project(0,6)
+    far(7)
+    grads(2)
+    project(6,7)
+    far(8)
+    project(7,9)
+    scan_start()
+    grads(3)
+    first_terms()
+    own_terms()
+    grads(4)
+    scan.prefix()
+    y_sums()
     grads(5)
+    adjoint_at = kept["adjoint"]
 
     rowsums = jnp.zeros((TOK, TOK), F32)
     colsums, ends, maps = [], [], []
@@ -563,30 +601,19 @@
             )
         return pair_sum, rowsums
 
-    for p in range(2):
-        pair_sum = jnp.zeros((TOK, TOK), F32)
-        pair_sum, rowsums = pairs(p, (0, 1, 2, 3), pair_sum, rowsums)
+    def pairs_of(p):
+        pair_sum, kept["rows"] = pairs(
+            p, (0, 1, 2, 3), jnp.zeros((TOK, TOK), F32), kept.get("rows", rowsums)
+        )
         maps.append(dot2(pair_sum, bs[p]))
-        if p == 0:
-            scan.prefix()
-    rowsums = rowsums.T[0 : 2 * HALF]
+
+    pairs_of(0)
+    pairs_of(1)
     grads(6)
     tcols.recv()
     each(1, chips, tcols_on.start_one)
-
-    def gather(first, last):
-        total = wtot[...] if first else jnp.zeros((CH, 2 * TOK), F32)
-        for d in range(first, last):
-            for way in (1, -1) if 0 < d < hops else (1,):
-                n = lax.rem(z + way * d + nz, nz)
-                grad = jnp.concatenate([ig[n, 0], ig[n, 1]], axis=1)
-                cols = [tcol[:, half, n].reshape(2 * TOK, TOK) for half in range(2)]
-                total = total + dot(grad, jnp.concatenate(cols, axis=1))
-        wtot[...] = total
-
     grads(7)
-    tcols_on.recv()
-    gather(0, hops)
+    rowsums = kept["rows"].T[0 : 2 * HALF]
 
     early = scan.result()
     state_at = [early, decay_rows[0] * early + s_first[...]]
@@ -611,6 +638,8 @@
 
     map_parts = Family(1, 4, map_to, m_in.at[pl.ds(1, 3)])
     map_parts.start()
+    tcols_on.recv()
+    gather(0, hops)
     grads(8)
     gather(hops, hops + 1)
     for half in range(2):
@@ -655,9 +684,9 @@
         total = total + y_in[j].astype(F32)
     token_grad[...] = total.astype(BF16)
     swap_s.wait_recv()
-    kept = jnp.where(low_half, s_out[0], s_out[1])
+    mixed = jnp.where(low_half, s_out[0], s_out[1])
     sub = lax.broadcasted_iota(jnp.int32, (2 * HALF, TOK), 0)
-    step_grad[...] = jnp.where((sub < HALF) == low_half, kept, s_swap[...])
+    step_grad[...] = jnp.where((sub < HALF) == low_half, mixed, s_swap[...])
     map_outs.recv()
     for n in range(2 * nk):
         rows = slice((n % 2) * (TOK // 2), (n % 2 + 1) * (TOK // 2))
@@ -767,20 +796,22 @@
     )(tokens, w, cot, b, c, raw, rate_log.reshape(1, 2 * HALF), skip.reshape(1, 2 * HALF))
 
     def hand_over(*refs):
-        copies = [
-            pltpu.make_async_copy(refs[n], refs[4 + n], refs[8].at[n]) for n in range(4)
-        ]
-        for copy in copies:
-            copy.start()
-        for copy in copies:
-            copy.wait()
+        for first in (0, 8):
+            copies = [
+                pltpu.make_async_copy(refs[(first + n) % 12], refs[8 - first // 2 + n], refs[12].at[n])
+                for n in range(4)
+            ]
+            for copy in copies:
+                copy.start()
+            for copy in copies:
+                copy.wait()
 
     return pl.pallas_call(
         hand_over,
         out_shape=tuple(jax.ShapeDtypeStruct(a.shape, a.dtype) for a in results),
         in_specs=[hbm] * 4,
         out_specs=(hbm,) * 4,
-        scratch_shapes=[pltpu.SemaphoreType.DMA((4,))],
+        scratch_shapes=[v(a.shape, a.dtype) for a in results] + [pltpu.SemaphoreType.DMA((4,))],
         compiler_params=pltpu.CompilerParams(vmem_limit_bytes=60 * 1024 * 1024),
         name="outputs",
     )(*results)

time: 122 us -> 101 us (0.83)
  Pallas kernels: 121 us -> 100 us
    pallas_call x1, Pallas kernels: 23.1 us -> 2.04 us  [local(): pl.pallas_call(hand_over, out_shape=tuple((jax.ShapeDtypeStruct(a.shape,...]
where the time goes in v5:
time: 101 us
  Pallas kernels  100 us (99%)
    pallas_call x1, Pallas kernels, local(): pl.pallas_call(body, out_shape=(jax.ShapeDtypeStruct((TOK, CH), BF16), ja...  98.2 us
    pallas_call x1, Pallas kernels, local(): pl.pallas_call(hand_over, out_shape=tuple((jax.ShapeDtypeStruct(a.shape,...  2.04 us

profile of v5, /device:TPU:1, one launch (start us, length us, event | category | flops | bytes accessed | tf_op | source)
XLA Modules:
  0.0 100.9 jit_solution(17378201987364608347)
XLA Ops:
  0.6 98.2 %mixer_backward.1 = (bf16[128,256]{1,0:T(8,128)(2,1)}, bf16[128,512]{1,0:T(8,128)(2,1)}, f32[8,128]{1,0:T(8,128)}, f32[8,128,128]{2,1,0:T(8,128)}) custom-call(bf16[128,256]{1,0:T(8,128)(2,1)} %refs_0_.1, bf16[128,512]{1,0:T(8,128)(2,1)} %refs_1_.1, bf16[128,512]{1,0:T(8,128)(2,1)} %refs_2_.1, bf16[8,128,128]{2,1,0:T(8,128)(2,1)} %refs_3_.1, ...), custom_call_target="tpu_custom_call" | custom-call | tf_op jit(solution)/shard_map/mixer_backward/pallas_call | solution.py:733
  98.8 2.0 %outputs.1 = (bf16[128,256]{1,0:T(8,128)(2,1)}, bf16[128,512]{1,0:T(8,128)(2,1)}, f32[8,128]{1,0:T(8,128)}, f32[8,128,128]{2,1,0:T(8,128)}) custom-call(bf16[128,256]{1,0:T(8,128)(2,1)} %get-tuple-element.8.refs_0_, bf16[128,512]{1,0:T(8,128)(2,1)} %get-tuple-element.9.refs_1_, f32[8,128]{1,0:T(8,128)} %get-tuple-element.10.refs_2_, ...), custom_call_target="tpu_custom_call" | custom-call | tf_op jit(solution)/shard_map/outputs/pallas_call | solution.py:809

commit v6 on v5

--- a/solution.py
+++ b/solution.py
@@ -81,6 +81,8 @@
     state_in,
     gte,
     gtb,
+    gt_high,
+    gt_low,
     xtb,
     dec,
     inter,
@@ -143,6 +145,9 @@
     def chip(j):
         return (r + j // nk) % 2, xor(k, j % nk, nk)
 
+    def far_first(j):
+        return hops + (1 - 2 * ((j - 1) % 2)) * (j // 2)
+
     sends, recvs = [0], [0]
 
     def take(counter, n=1):
@@ -351,7 +356,7 @@
     dall[z] = decay_row
 
     def decay_out(j):
-        return dtile, dall.at[z], ztok(z + j, r), c
+        return dtile, dall.at[z], ztok(z + far_first(j), r), c
 
     decays = Family(1, nz, decay_out, dall.at[pl.ds(0, nz - 1)])
     decays.start()
@@ -373,11 +378,11 @@
             self.n, self.reverse = n, reverse
 
             def out(j):
-                to = lax.rem(z + j, nz)
+                to = lax.rem(z + far_first(j), nz)
                 return send_state.at[n, to], recv_state.at[n, z], ztok(to, r), c
 
             def back(j):
-                to = lax.rem(z + j, nz)
+                to = lax.rem(z + far_first(j), nz)
                 return back_state.at[n, to], state_in.at[n, z], ztok(to, r), c
 
             self.out = Family(1, nz, out, recv_state.at[n, pl.ds(0, nz - 1)])
@@ -433,7 +438,7 @@
     kept = {}
 
     def column_out(j):
-        to = lax.rem(z + j, nz)
+        to = lax.rem(z + far_first(j), nz)
         return tpre.at[to], tcol.at[me, core, z], ztok(to, r), c
 
     def tcol_out(j):
@@ -606,6 +611,9 @@
             p, (0, 1, 2, 3), jnp.zeros((TOK, TOK), F32), kept.get("rows", rowsums)
         )
         maps.append(dot2(pair_sum, bs[p]))
+        turned = gte[p].T
+        gt_high[p] = turned.astype(BF16)
+        gt_low[p] = (turned - gt_high[p].astype(F32)).astype(BF16)
 
     pairs_of(0)
     pairs_of(1)
@@ -617,11 +625,22 @@
 
     early = scan.result()
     state_at = [early, decay_rows[0] * early + s_first[...]]
+    for p in range(2):
+        low_state = state_at[p].astype(BF16)
+        maps[p] = maps[p] + (dot(gt_high[p], low_state) + dot(gt_low[p], low_state))
+        m_own[p] = maps[p].reshape(2, TOK // 2, STATE)
+
+    def map_to(j):
+        rr, cc = (r + j // 2) % 2, (core + j % 2) % 2
+        return m_own.at[rr, cc], m_in.at[j], z * 2 + rr, 2 * k + cc
+
+    map_parts = Family(1, 4, map_to, m_in.at[pl.ds(1, 3)])
+    map_parts.start()
+
     starts, corners = [], []
     for p in range(2):
         at_c = dot2(state_at[p], cs[p], NT)
         gs = gte[p]
-        maps[p] = maps[p] + dot2(gs.T, state_at[p].astype(BF16))
         meets = adjoint_at[p] * state_at[p]
         for i in range(HALF):
             span = slice(i * HEAD, (i + 1) * HEAD)
@@ -630,23 +649,6 @@
             corners.append(
                 jnp.broadcast_to(jnp.sum(lanes, axis=1, keepdims=True), (1, TOK))
             )
-        m_own[p] = maps[p].reshape(2, TOK // 2, STATE)
-
-    def map_to(j):
-        rr, cc = (r + j // 2) % 2, (core + j % 2) % 2
-        return m_own.at[rr, cc], m_in.at[j], z * 2 + rr, 2 * k + cc
-
-    map_parts = Family(1, 4, map_to, m_in.at[pl.ds(1, 3)])
-    map_parts.start()
-    tcols_on.recv()
-    gather(0, hops)
-    grads(8)
-    gather(hops, hops + 1)
-    for half in range(2):
-        wgrad[half] = wtot[:, half * TOK : (half + 1) * TOK].T.astype(BF16)
-    swap_o = single(wgrad.at[1 - r], weight_grad.at[:, mine], partner, c)
-    swap_o.start()
-    weight_grad[:, mine] = wgrad[r]
 
     for n, parts in enumerate((colsums, ends, starts, corners)):
         for q in range(2 * HALF):
@@ -661,14 +663,16 @@
         + block_decay * corner
     )
     sigmoid = 1.0 / (1.0 + jnp.exp(-raw8))
-    grads = sigmoid * (input_term + rates * decay_term)
-    s_out[0, 0:HALF, :] = grads[0:HALF]
-    s_out[0, HALF : 2 * HALF, :] = grads[0:HALF]
-    s_out[1, 0:HALF, :] = grads[HALF : 2 * HALF]
-    s_out[1, HALF : 2 * HALF, :] = grads[HALF : 2 * HALF]
+    step_terms = sigmoid * (input_term + rates * decay_term)
+    s_out[0, 0:HALF, :] = step_terms[0:HALF]
+    s_out[0, HALF : 2 * HALF, :] = step_terms[0:HALF]
+    s_out[1, 0:HALF, :] = step_terms[HALF : 2 * HALF]
+    s_out[1, HALF : 2 * HALF, :] = step_terms[HALF : 2 * HALF]
     swap_s = single(s_out.at[1 - r], s_swap, partner, c)
     swap_s.start()
 
+    tcols_on.recv()
+    gather(0, hops)
     map_parts.recv()
     m_groups[c] = (m_own[r, core] + m_in[1] + m_in[2] + m_in[3]).astype(BF16)
 
@@ -677,6 +681,14 @@
 
     map_outs = Family(1, 2 * nk, map_out, m_groups.at[pl.ds(0, 2 * nk - 1)])
     map_outs.start()
+
+    grads(8)
+    gather(hops, hops + 1)
+    for half in range(2):
+        wgrad[half] = wtot[:, half * TOK : (half + 1) * TOK].T.astype(BF16)
+    swap_o = single(wgrad.at[1 - r], weight_grad.at[:, mine], partner, c)
+    swap_o.start()
+    weight_grad[:, mine] = wgrad[r]
 
     y_outs.recv()
     total = y_in[0].astype(F32)
@@ -764,6 +776,8 @@
             v((2, nz, piece, STATE), BF16),
             v((2, CH, TOK), F32),
             v((2, CH, TOK), BF16),
+            v((2, TOK, CH), BF16),
+            v((2, TOK, CH), BF16),
             v((2, CH, TOK), BF16),
             v((2 * HALF, TOK, TOK), F32),
             v((2, TOK, TOK), F32),

time: 101 us -> 100 us (0.990)
  no operation moved by 1% of the time
where the time goes in v6:
time: 100 us; the launch traced here: 99.9 us
  Pallas kernels  99.3 us (99%)
    pallas_call x1, Pallas kernels, local(): pl.pallas_call(body, out_shape=(jax.ShapeDtypeStruct((TOK, CH), BF16), ja...  97.3 us
    pallas_call x1, Pallas kernels, local(): pl.pallas_call(hand_over, out_shape=tuple((jax.ShapeDtypeStruct(a.shape,...  2.04 us

profile of v6, /device:TPU:1, one launch (start us, length us, event | category | flops | bytes accessed | tf_op | source)
XLA Modules:
  0.0 99.9 jit_solution(10666131073016182498)
XLA Ops:
  0.6 97.3 %mixer_backward.1 = (bf16[128,256]{1,0:T(8,128)(2,1)}, bf16[128,512]{1,0:T(8,128)(2,1)}, f32[8,128]{1,0:T(8,128)}, f32[8,128,128]{2,1,0:T(8,128)}) custom-call(bf16[128,256]{1,0:T(8,128)(2,1)} %refs_0_.1, bf16[128,512]{1,0:T(8,128)(2,1)} %refs_1_.1, bf16[128,512]{1,0:T(8,128)(2,1)} %refs_2_.1, bf16[8,128,128]{2,1,0:T(8,128)(2,1)} %refs_3_.1, ...), custom_call_target="tpu_custom_call" | custom-call | tf_op jit(solution)/shard_map/mixer_backward/pallas_call | solution.py:745
  97.9 2.0 %outputs.1 = (bf16[128,256]{1,0:T(8,128)(2,1)}, bf16[128,512]{1,0:T(8,128)(2,1)}, f32[8,128]{1,0:T(8,128)}, f32[8,128,128]{2,1,0:T(8,128)}) custom-call(bf16[128,256]{1,0:T(8,128)(2,1)} %get-tuple-element.8.refs_0_, bf16[128,512]{1,0:T(8,128)(2,1)} %get-tuple-element.9.refs_1_, f32[8,128]{1,0:T(8,128)} %get-tuple-element.10.refs_2_, ...), custom_call_target="tpu_custom_call" | custom-call | tf_op jit(solution)/shard_map/outputs/pallas_call | solution.py:823
